TPU v7x, 256 devices: a whole 4x4x8 slice. The times are simulated.
256 devices in a mesh: row: 16 (over x, z_hi), col: 16 (over z_lo, y, core).
Axes of the slice: x: 4, y: 4, z: 8 (z_hi: 4, z_lo: 2; z = z_hi * 2 + z_lo), core: 2. Of those that a mesh axis runs over, the one named last changes fastest.
Arguments:
- pair: bfloat16 [512, 512, 128], P('row', 'col'), may hold values from -6 to 6
- pair_mask: int32 [512, 512], P('row', 'col'), may hold values 0 or 1
- norm_in_gain: float32 [2, 128], replicated, may hold values from 0.5 to 1.5
- norm_in_bias: float32 [2, 128], replicated, may hold values from -3 to 3
- proj_weight: bfloat16 [2, 128, 256], replicated, may hold values from -0.5 to 0.5
- proj_gate: bfloat16 [2, 128, 256], replicated, may hold values from -0.5 to 0.5
- out_gate: bfloat16 [2, 128, 128], replicated, may hold values from -0.5 to 0.5
- norm_out_gain: float32 [2, 128], replicated, may hold values from 0.5 to 1.5
- norm_out_bias: float32 [2, 128], replicated, may hold values from -3 to 3
- out_weight: bfloat16 [2, 128, 128], replicated, may hold values from -0.5 to 0.5
Outputs:
- updated: bfloat16 [512, 512, 128], P('row', 'col')
All inputs are finite; a program needn't handle non-finite values. No bound on the sum of `pair_mask` on one device may be relied on, other than what follows from the above.
Results may differ from a plain program's by a relative error of at most 0.015.
Values may be sent and summed in bfloat16 or wider, within the bound.
No kernel may reach another device: no remote copies, remote signals or barrier semaphores. Data moves between devices by JAX's collectives and lax.ppermute only.
A program may use at most 128 MiB of HBM per device.

v0:
```python
import jax
import jax.numpy as jnp
from jax import lax
from jax.sharding import PartitionSpec as P

C = 128


def layer_norm(values, gain_vec, bias_vec):
    average = jnp.mean(values, axis=-1, keepdims=True)
    centered = values - average
    variance = jnp.mean(centered * centered, axis=-1, keepdims=True)
    return centered * lax.rsqrt(variance + 1e-05) * gain_vec + bias_vec


def outgoing_partials(left_side, right_side):
    gathered = lax.all_gather(right_side, "row", axis=0, tiled=True)
    summed = lax.psum_scatter(
        jnp.einsum("ikc,jkc->jic", left_side, gathered, preferred_element_type=jnp.float32).astype(
            jnp.bfloat16
        ),
        "col",
        scatter_dimension=0,
        tiled=True,
    ).astype(jnp.float32)
    return jnp.transpose(summed, (1, 0, 2))


def incoming_partials(left_side, right_side):
    gathered = lax.all_gather(left_side, "col", axis=1, tiled=True)
    return lax.psum_scatter(
        jnp.einsum("kic,kjc->ijc", gathered, right_side, preferred_element_type=jnp.float32).astype(
            jnp.bfloat16
        ),
        "row",
        scatter_dimension=0,
        tiled=True,
    ).astype(jnp.float32)


def triangle(pair, mask_float, layer_index, outgoing, params):
    (
        norm_in_gain,
        norm_in_bias,
        proj_weight,
        proj_gate,
        out_gate,
        norm_out_gain,
        norm_out_bias,
        out_weight,
    ) = params
    pair_float = pair.astype(jnp.float32)
    normed = layer_norm(pair_float, norm_in_gain[layer_index], norm_in_bias[layer_index]).astype(
        jnp.bfloat16
    )
    projected = jnp.dot(normed, proj_weight[layer_index], preferred_element_type=jnp.float32)
    gate_proj = jnp.dot(normed, proj_gate[layer_index], preferred_element_type=jnp.float32)
    operands = (jax.nn.sigmoid(gate_proj) * projected * mask_float).astype(jnp.bfloat16)
    left_side = operands[..., :C]
    right_side = operands[..., C:]
    if outgoing:
        product = outgoing_partials(left_side, right_side)
    else:
        product = incoming_partials(left_side, right_side)
    product_normed = layer_norm(
        product, norm_out_gain[layer_index], norm_out_bias[layer_index]
    ).astype(jnp.bfloat16)
    out_gated = jax.nn.sigmoid(
        jnp.dot(normed, out_gate[layer_index], preferred_element_type=jnp.float32)
    )
    update = out_gated * jnp.dot(
        product_normed, out_weight[layer_index], preferred_element_type=jnp.float32
    )
    return (pair_float + update).astype(jnp.bfloat16)


def on_device(
    pair,
    pair_mask,
    norm_in_gain,
    norm_in_bias,
    proj_weight,
    proj_gate,
    out_gate,
    norm_out_gain,
    norm_out_bias,
    out_weight,
):
    params = (
        norm_in_gain,
        norm_in_bias,
        proj_weight,
        proj_gate,
        out_gate,
        norm_out_gain,
        norm_out_bias,
        out_weight,
    )
    mask_float = pair_mask.astype(jnp.float32)[..., None]
    first_pass = triangle(pair, mask_float, 0, True, params)
    return triangle(first_pass, mask_float, 1, False, params)


def solution(mesh):
    in_specs = (P("row", "col", None), P("row", "col"), P(), P(), P(), P(), P(), P(), P(), P())
    out_specs = P("row", "col", None)
    return jax.shard_map(
        on_device, mesh=mesh, in_specs=in_specs, out_specs=out_specs, check_vma=False
    )
```

profile of v0, /device:TPU:1, one launch (start us, length us, event | category | flops | bytes accessed | tf_op | source)
XLA Modules:
  0.0 379.9 jit_solution(7843020488445637222)
XLA Ops:
  6.5 1.2 convert_reduce_fusion
  7.7 1.3 fusion.27
  9.1 0.7 convert_element_type.51
  9.8 0.8 slice_bitcast_fusion.2
  10.5 1.4 fusion.50
  12.0 1.4 fusion.11
  13.4 0.8 fusion.69
  14.2 0.0 all-gather.3.cloned.1.call-update
  14.2 0.0 reduce-scatter.3.cloned.1.call-start
  14.3 1.4 copy.48
  15.7 77.2 %all-gather.3.cloned.1.call-done = bf16[512,32,128]{2,1,0:T(8,128)(2,1)} async-done(((bf16[32,32,128]{2,1,0:T(8,128)(2,1)}), bf16[512,32,128]{2,1,0:T(8,128)(2,1)}) %all-gather.3.cloned.1.call-update) | async-done | bytes 4194320 | tf_op jit(solution)/shard_map/all_gather | solution.py:17
  92.9 23.0 %copy.47 = bf16[512,32,128]{1,0,2:T(8,128)(2,1)} copy(bf16[512,32,128]{2,1,0:T(8,128)(2,1)} %all-gather.3.cloned.1.call-done) | data formatting | bytes 8388608 | tf_op jit(solution)/shard_map/all_gather | solution.py:17
  115.9 10.7 %convert_bitcast_fusion.1 = bf16[512,32,128]{0,1,2:T(8,128)(2,1)} fusion(bf16[512,32,128]{1,0,2:T(8,128)(2,1)} %copy.47, bf16[32,32,128]{1,0,2:T(8,128)(2,1)S(1)} %copy.48), kind=kOutput, calls=%fused_computation.1 | convolution fusion | flops 136314880 | bytes 8650752 | tf_op jit(solution)/shard_map/ikc,jkc->jic/dot_general | solution.py:19
  126.6 9.1 %copy.49 = bf16[512,32,128]{2,1,0:T(8,128)(2,1)} copy(bf16[512,32,128]{0,1,2:T(8,128)(2,1)} %convert_bitcast_fusion.1) | data formatting | bytes 8388608 | tf_op jit(solution)/shard_map/convert_element_type | solution.py:19
  135.8 0.0 copy-start.2
  135.8 0.0 reduce-scatter.3.cloned.1.call-update
  135.8 0.0 all-gather.5.cloned.1.call-start
  135.9 0.6 copy-done.3
  136.5 0.0 copy-done.4
  136.5 0.3 copy-done
  136.8 0.5 fusion.17
  137.2 65.5 %reduce-scatter.3.cloned.1.call-done = bf16[32,32,128]{2,1,0:T(8,128)(2,1)} async-done(((bf16[512,32,128]{2,1,0:T(8,128)(2,1)}), bf16[32,32,128]{2,1,0:T(8,128)(2,1)}) %reduce-scatter.3.cloned.1.call-update) | async-done | bytes 262160 | tf_op jit(solution)/shard_map/reduce_scatter | solution.py:18
  202.8 1.2 bitcast_reduce_fusion
  203.9 0.1 copy.50
  204.0 0.1 copy.51
  204.1 1.3 fusion.37
  205.4 0.1 copy.52
  205.5 0.1 copy.53
  205.6 1.3 fusion.40
  206.9 0.4 fusion.70
  207.3 0.4 multiply_reduce_fusion
  207.7 0.3 add_convert_fusion
  208.0 0.3 fusion.47
  208.3 0.4 fusion.10
  208.8 0.8 fusion.68
  209.6 0.0 all-gather.5.cloned.1.call-update
  209.6 0.2 reduce-scatter.5.cloned.1.call-start
  209.8 1.6 copy.55
  211.4 40.2 %all-gather.5.cloned.1.call-done = bf16[32,512,128]{2,1,0:T(8,128)(2,1)} async-done(((bf16[32,32,128]{2,1,0:T(8,128)(2,1)}), bf16[32,512,128]{2,1,0:T(8,128)(2,1)}) %all-gather.5.cloned.1.call-update) | async-done | bytes 4194320 | tf_op jit(solution)/shard_map/all_gather | solution.py:30
  251.7 8.0 %copy.56 = bf16[32,512,128]{1,0,2:T(8,128)(2,1)} copy(bf16[32,512,128]{2,1,0:T(8,128)(2,1)} %all-gather.5.cloned.1.call-done) | data formatting | bytes 8388608 | tf_op jit(solution)/shard_map/all_gather | solution.py:30
  259.6 5.4 %convert_bitcast_fusion = bf16[512,32,128]{0,1,2:T(8,128)(2,1)} fusion(bf16[32,32,128]{0,1,2:T(8,128)(2,1)S(1)} %copy.55, bf16[32,512,128]{1,0,2:T(8,128)(2,1)} %copy.56), kind=kOutput, calls=%fused_computation | convolution fusion | flops 136314880 | bytes 8650752 | tf_op jit(solution)/shard_map/kic,kjc->ijc/dot_general | solution.py:32
  265.0 9.1 %copy.57 = bf16[512,32,128]{2,1,0:T(8,128)(2,1)} copy(bf16[512,32,128]{0,1,2:T(8,128)(2,1)} %convert_bitcast_fusion) | data formatting | bytes 8388608 | tf_op jit(solution)/shard_map/convert_element_type | solution.py:32
  274.2 0.0 reduce-scatter.5.cloned.1.call-update
  274.2 0.3 fusion.14
  274.5 94.2 %reduce-scatter.5.cloned.1.call-done = bf16[32,32,128]{2,1,0:T(8,128)(2,1)} async-done(((bf16[512,32,128]{2,1,0:T(8,128)(2,1)}), bf16[32,32,128]{2,1,0:T(8,128)(2,1)}) %reduce-scatter.5.cloned.1.call-update) | async-done | bytes 262160 | tf_op jit(solution)/shard_map/reduce_scatter | solution.py:31
  368.7 1.2 convert_reduce_fusion.1
  369.9 1.3 fusion.31
  371.2 2.1 fusion.20
  (20 shorter events, 0.1 us)
Async XLA Ops:
  6.5 86.4 %all-gather.3.cloned.1.call-start = ((), (), s32[]{:S(2)}) async-start(), calls=%async_computation.2 | async-start | bytes 4456448 | tf_op jit(solution)/shard_map/all_gather | solution.py:17
  14.2 188.5 %reduce-scatter.3.cloned.1.call-start = ((), (), s32[]{:S(2)}) async-start(), calls=%async_computation.3 | async-start | bytes 4456448 | tf_op jit(solution)/shard_map/reduce_scatter | solution.py:18
  135.8 0.7 copy-start.3
  135.8 0.7 copy-start.4
  135.8 1.0 copy-start
  135.8 1.0 copy-start.6
  135.8 71.1 %copy-start.2 = (bf16[2,128,128]{2,1,0:T(8,128)(2,1)S(1)}, bf16[2,128,128]{2,1,0:T(8,128)(2,1)}, u32[]{:S(2)}) copy-start(bf16[2,128,128]{2,1,0:T(8,128)(2,1)} %param.19) | copy-start | bytes 196612
  135.8 72.2 %copy-start.1 = (bf16[2,128,256]{2,1,0:T(8,128)(2,1)S(1)}, bf16[2,128,256]{2,1,0:T(8,128)(2,1)}, u32[]{:S(2)}) copy-start(bf16[2,128,256]{2,1,0:T(8,128)(2,1)} %param.14) | copy-start | bytes 393220
  135.8 115.8 %all-gather.5.cloned.1.call-start = ((), (), s32[]{:S(2)}) async-start(), calls=%async_computation.4 | async-start | bytes 4456448 | tf_op jit(solution)/shard_map/all_gather | solution.py:30
  136.8 71.5 %copy-start.5 = (bf16[2,128,256]{2,1,0:T(8,128)(2,1)S(1)}, bf16[2,128,256]{2,1,0:T(8,128)(2,1)}, u32[]{:S(2)}) copy-start(bf16[2,128,256]{2,1,0:T(8,128)(2,1)} %param.15) | copy-start | bytes 393220
  209.6 159.1 %reduce-scatter.5.cloned.1.call-start = ((), (), s32[]{:S(2)}) async-start(), calls=%async_computation.5 | async-start | bytes 4456448 | tf_op jit(solution)/shard_map/reduce_scatter | solution.py:31
Sparse Core Ops, SparseCore 0:
  14.4 78.4 all-gather.2
  135.9 66.7 reduce-scatter.2
  209.7 41.9 all-gather.4
  274.3 94.3 reduce-scatter.4
where the time goes:
time: 381 us; the launch traced here: 380 us
  waiting for transfers between devices  277 us (73%)
  local copies, waits for them, and re-layouts  55.9 us (15%)
  matrix products  22.9 us (6%)
  between operations  13.3 us (3%)
  other arithmetic  10.3 us (3%)
    reduce_scatter x1, waiting for transfers between devices, incoming_partials(): lax.psum_scatter(jnp.einsum('kic,kjc->ijc', gathered, right_side, preferr...  94.2 us
    all_gather x1, waiting for transfers between devices, outgoing_partials(): gathered = lax.all_gather(right_side, 'row', axis=0, tiled=True)  77.2 us
    reduce_scatter x1, waiting for transfers between devices, outgoing_partials(): lax.psum_scatter(jnp.einsum('ikc,jkc->jic', left_side, gathered, preferre...  65.5 us
    all_gather x1, waiting for transfers between devices, incoming_partials(): gathered = lax.all_gather(left_side, 'col', axis=1, tiled=True)  40.2 us
    all_gather x1, local copies, waits for them, and re-layouts, outgoing_partials(): gathered = lax.all_gather(right_side, 'row', axis=0, tiled=True)  23 us
    dot_general x1, matrix products, outgoing_partials(): jnp.einsum('ikc,jkc->jic', left_side, gathered, preferred_element_type=jn...  10.7 us
    convert_element_type x1, local copies, waits for them, and re-layouts, outgoing_partials(): jnp.einsum('ikc,jkc->jic', left_side, gathered, preferred_element_type=jn...  9.13 us
    convert_element_type x1, local copies, waits for them, and re-layouts, incoming_partials(): jnp.einsum('kic,kjc->ijc', gathered, right_side, preferred_element_type=j...  9.13 us
  transfers between devices with their start and end apart: 4, of which 4 were waited for; matrix products, arithmetic and copies ran while one was open for 1% of the time, Pallas kernels for 0%

commit v1 on v0

v1 whole, which is shorter than its diff:
```python
import jax
import jax.numpy as jnp
from jax import lax
from jax.experimental import pallas as pl
from jax.experimental.pallas import tpu as pltpu
from jax.sharding import Mesh
from jax.sharding import PartitionSpec as P

C = 128
T = 32
F32 = jnp.float32
BF16 = jnp.bfloat16
CHIPS = ("x", "zh", "zl", "y")
VMEM_LIMIT = 32 * 1024 * 1024


def dot(a, b):
    return jnp.dot(a, b, preferred_element_type=F32)


def dot_nt(a, b):
    return lax.dot_general(a, b, (((1,), (1,)), ((), ())), preferred_element_type=F32)


def sigmoid(v):
    return 0.5 * jnp.tanh(0.5 * v) + 0.5


def layer_norm_lanes(values, gain, bias):
    average = jnp.mean(values, axis=-1, keepdims=True)
    centered = values - average
    variance = jnp.mean(centered * centered, axis=-1, keepdims=True)
    return centered * lax.rsqrt(variance + 1e-05) * gain + bias


def iota(shape, dim):
    return lax.broadcasted_iota(jnp.int32, shape, dim)


def group_select(rows):
    group = iota((8, C), 1) // T
    out = rows[0:8]
    for q in range(1, 4):
        out = jnp.where(group == q, rows[8 * q : 8 * q + 8], out)
    return out


def swap_groups():
    src = iota((4 * C, 4 * C), 0)
    dst = iota((4 * C, 4 * C), 1)
    back = (dst & (T - 1)) | (((dst >> 5) & 3) << 7) | ((dst >> 7) << 5)
    return jnp.where(src == back, 1.0, 0.0).astype(BF16)


def emit_operands(normed, mask_row, weight_t, gate_t, scratch, s):
    projected = dot_nt(weight_t, normed)
    gate = dot_nt(gate_t, normed)
    operands = sigmoid(gate) * projected * mask_row
    scratch[pl.ds(s, C, stride=16), :] = operands[:C]
    scratch[pl.ds(8 + s, C, stride=16), :] = operands[C:]


def first_kernel(pair, mask, gain, bias, weight, gate, out_gate, lr, g_out, scratch):
    weight_t = weight[0].T
    gate_t = gate[0].T
    wide = jnp.where((iota((T, C), 1) & (T - 1)) == iota((T, C), 0), 1.0, 0.0).astype(BF16)
    mask_rows = group_select(dot(mask[...].astype(F32).astype(BF16), wide))
    for s in range(8):
        x = jnp.concatenate([pair[8 * q + s].astype(F32) for q in range(4)], axis=0)
        normed = layer_norm_lanes(x, gain[0:1, :], bias[0:1, :]).astype(BF16)
        opened = sigmoid(dot(normed, out_gate[0]))
        for q in range(4):
            g_out[pl.ds((8 * q + s) * T, T), :] = opened[q * T : (q + 1) * T]
        emit_operands(normed, mask_rows[s : s + 1], weight_t, gate_t, scratch, s)
    lr[...] = scratch[...].reshape(C, 16, C).astype(BF16)


def product_normed_rows(y, gain, bias, scratch, layer):
    values = y[...].astype(F32)
    average = jnp.mean(values, axis=0, keepdims=True)
    centered = values - average
    variance = jnp.mean(centered * centered, axis=0, keepdims=True)
    scratch[...] = (centered * lax.rsqrt(variance + 1e-05)).reshape(8 * C, C)
    gain_full = jnp.broadcast_to(gain[layer : layer + 1, :], (C, C)).T
    bias_full = jnp.broadcast_to(bias[layer : layer + 1, :], (C, C)).T
    return gain_full, bias_full


def update_rows(scratch, s, gain_full, bias_full, weight):
    normed = scratch[pl.ds(s, C, stride=8), :] * gain_full + bias_full
    return dot(normed.T.astype(BF16), weight)


def middle_kernel(
    y, pair, g_in, mask, in_gain, in_bias, weight, gate, out_gate, out_gain, out_bias, out_weight,
    lr, z_out, g_out, scratch, scratch_y, scratch_z,
):
    weight_t = weight[1].T
    gate_t = gate[1].T
    four = jnp.concatenate([mask[...].astype(F32).astype(BF16)] * 4, axis=0)
    eye = jnp.where(iota((T, T), 1) == iota((T, T), 0), 1.0, 0.0).astype(BF16)
    mask_rows = group_select(dot_nt(eye, four))
    scratch_z[...] = pair[...].astype(F32).reshape(T * T, C)
    gain_full, bias_full = product_normed_rows(y, out_gain, out_bias, scratch_y, 0)
    for s in range(8):
        update = update_rows(scratch_y, s, gain_full, bias_full, out_weight[0])
        rows = [pl.ds(8 * q + s, T, stride=T) for q in range(4)]
        z = jnp.concatenate([scratch_z[r, :] for r in rows], axis=0)
        g = jnp.concatenate([g_in[r, :] for r in rows], axis=0)
        z = (z + g * update).astype(BF16).astype(F32)
        normed = layer_norm_lanes(z, in_gain[1:2, :], in_bias[1:2, :]).astype(BF16)
        opened = sigmoid(dot(normed, out_gate[1]))
        for q in range(4):
            z_out[rows[q], :] = z[q * T : (q + 1) * T]
            g_out[rows[q], :] = opened[q * T : (q + 1) * T]
        emit_operands(normed, mask_rows[s : s + 1], weight_t, gate_t, scratch, s)
    lr[...] = scratch[...].reshape(C, 16, C).astype(BF16)


def last_kernel(y, z_in, g_in, out_gain, out_bias, out_weight, out, scratch_y):
    gain_full, bias_full = product_normed_rows(y, out_gain, out_bias, scratch_y, 1)
    for s in range(8):
        update = update_rows(scratch_y, s, gain_full, bias_full, out_weight[1])
        for q in range(4):
            rows = pl.ds((8 * q + s) * T, T)
            piece = z_in[rows, :] + g_in[rows, :] * update[q * T : (q + 1) * T]
            out[8 * q + s] = piece.astype(BF16)


def outgoing_kernel(core, own, other, out, left, right):
    swap = swap_groups()
    half = core[0]
    for part, src in enumerate((own, other)):
        for quad in range(2):
            y = jnp.concatenate(
                [src[:, 4 * quad + c].reshape(256, C) for c in range(4)], axis=1
            )
            z = dot(y, swap).reshape(16, 16, 4 * C)
            depth = pl.ds((2 * part + quad) * C, C)
            for q in range(4):
                left[:, q, :, depth] = z[:, :8, q * C : (q + 1) * C]
                right[:, q, :, depth] = z[:, 8:, q * C : (q + 1) * C]
    a = left[...].reshape(512, 512).astype(BF16)
    pairs = right.reshape(8, 2, 4, 8, 512)
    b = jnp.concatenate([pairs[:, half, q].reshape(64, 512) for q in range(4)], axis=0)
    product = dot_nt(b.astype(BF16), a).astype(BF16)
    for quad in range(4):
        y = jnp.concatenate(
            [product[64 * q : 64 * q + 64, quad * C : (quad + 1) * C] for q in range(4)], axis=1
        )
        z = dot(y, swap)
        for r in range(4):
            out[4 * quad + r] = z[:, r * C : (r + 1) * C].reshape(8, 8, C).astype(BF16)


def incoming_kernel(core, own, other, out, left, right):
    swap = swap_groups()
    half = core[0]
    for part, src in enumerate((own, other)):
        for quad in range(4):
            y = jnp.concatenate([src[4 * quad + r].reshape(C, C) for r in range(4)], axis=1)
            z = dot(y, swap).reshape(8, 16, 4 * C)
            depth = pl.ds(quad * C, C)
            for q in range(4):
                left[q, part, :, :, depth] = z[:, :8, q * C : (q + 1) * C]
                if part == 0:
                    right[:, q, :, depth] = z[:, 8:, q * C : (q + 1) * C]
    a = left[...].reshape(512, 512).astype(BF16)
    b = right[...].reshape(256, 512).astype(BF16)
    product = dot_nt(a, b).astype(BF16)
    for quad in range(2):
        y = jnp.concatenate(
            [product[C * q : C * q + C, quad * C : (quad + 1) * C] for q in range(4)], axis=1
        )
        z = dot(y, swap)
        for c in range(4):
            piece = z[:, c * C : (c + 1) * C].reshape(2, 8, 8, C).astype(BF16)
            out[:, half, 4 * quad + c] = piece[0]
            out[:, 1 - half, 4 * quad + c] = piece[1]


def call(kernel, out_shape, scratch, *args, smem=0):
    vmem = pl.BlockSpec(memory_space=pltpu.VMEM)
    scalars = pl.BlockSpec(memory_space=pltpu.SMEM)
    return pl.pallas_call(
        kernel,
        out_shape=out_shape,
        in_specs=[scalars] * smem + [vmem] * (len(args) - smem),
        out_specs=[vmem] * len(out_shape) if isinstance(out_shape, list) else vmem,
        scratch_shapes=[pltpu.VMEM(shape, F32) for shape in scratch],
        compiler_params=pltpu.CompilerParams(vmem_limit_bytes=VMEM_LIMIT),
    )(*args)


def struct(shape, dtype):
    return jax.ShapeDtypeStruct(shape, dtype)


def exchange(values):
    return lax.all_to_all(values, CHIPS, 0, 0)


def other_core(values):
    return lax.ppermute(values, "core", [(0, 1), (1, 0)])


def on_device(
    pair, pair_mask, in_gain, in_bias, weight, gate, out_gate, out_gain, out_bias, out_weight
):
    core = lax.axis_index("core").astype(jnp.int32).reshape(1)
    operands = struct((C, 16, C), BF16)
    rows = struct((T * T, C), F32)
    lr, g = call(
        first_kernel, [operands, rows], [(16 * C, C)],
        pair, pair_mask, in_gain, in_bias, weight, gate, out_gate,
    )
    own = exchange(lr)
    other = other_core(own)
    y = call(
        outgoing_kernel, struct((16, 8, 8, C), BF16), [(16, 4, 8, 512), (16, 4, 8, 512)],
        core, own.reshape(16, 8, 16, C), other.reshape(16, 8, 16, C), smem=1,
    )
    y = exchange(y.reshape(C, 8, C))
    lr, z, g = call(
        middle_kernel, [operands, rows, rows], [(16 * C, C), (8 * C, C), (T * T, C)],
        y, pair, g, pair_mask, in_gain, in_bias, weight, gate, out_gate, out_gain, out_bias,
        out_weight,
    )
    own = exchange(lr)
    other = other_core(own)
    y = call(
        incoming_kernel, struct((8, 2, 8, 8, C), BF16), [(4, 2, 8, 8, 512), (8, 4, 8, 512)],
        core, own.reshape(16, 8, 16, C), other.reshape(16, 8, 16, C), smem=1,
    )
    y = exchange(y.reshape(C, 8, C))
    return call(
        last_kernel, struct((T, T, C), BF16), [(8 * C, C)],
        y, z, g, out_gain, out_bias, out_weight,
    )


def solution(mesh):
    chips = Mesh(mesh.devices.reshape(4, 4, 2, 4, 2), CHIPS + ("core",))
    tile = P(("x", "zh"), ("zl", "y", "core"))
    return jax.shard_map(
        on_device,
        mesh=chips,
        in_specs=(tile, tile) + (P(),) * 8,
        out_specs=tile,
        check_vma=False,
    )
```

time: 381 us -> 123 us (0.32)
  waiting for transfers between devices: 277 us -> 3.07 us
  blocking collectives: 0 us -> 94.7 us
  local copies, waits for them, and re-layouts: 55.9 us -> 6.32 us
  matrix products: 22.9 us -> 0 us
  between operations: 13.3 us -> 0.14 us
  other arithmetic: 10.3 us -> 0 us
  Pallas kernels: 0 us -> 10.1 us
  starting transfers between devices: 0.31 us -> 7.78 us
    reduce_scatter x2 -> x0, waiting for transfers between devices: 160 us -> none  [the longest x1 94.2 us: incoming_partials(): lax.psum_scatter(jnp.einsum('kic,kjc->ijc', gathered, right_side, preferr...]
    all_gather x2 -> x0, waiting for transfers between devices: 117 us -> none  [the longest x1 77.2 us: outgoing_partials(): gathered = lax.all_gather(right_side, 'row', axis=0, tiled=True)]
    all_to_all x0 -> x4, blocking collectives: none -> 94.7 us  [exchange(): return lax.all_to_all(values, CHIPS, 0, 0)]
    all_gather x2 -> x0, local copies, waits for them, and re-layouts: 31 us -> none  [the longest x1 23 us: outgoing_partials(): gathered = lax.all_gather(right_side, 'row', axis=0, tiled=True)]
    dot_general x10 -> x0, matrix products: 22.9 us -> none  [the longest x1 10.7 us: outgoing_partials(): jnp.einsum('ikc,jkc->jic', left_side, gathered, preferred_element_type=jn...]
    convert_element_type x2 -> x0, local copies, waits for them, and re-layouts: 18.3 us -> none  [the longest x1 9.13 us: outgoing_partials(): jnp.einsum('ikc,jkc->jic', left_side, gathered, preferred_element_type=jn...]
    pallas_call x0 -> x5, Pallas kernels: none -> 10.1 us  [call(): pl.pallas_call(kernel, out_shape=out_shape, in_specs=[scalars] * smem + [...]
    reduce_sum x7 -> x0, other arithmetic: 7.84 us -> none  [the longest x4 4.37 us: layer_norm(): variance = jnp.mean(centered * centered, axis=-1, keepdims=True)]
  transfers between devices with their start and end apart: 4 -> 2, of which waited for: 4 -> 2; matrix products, arithmetic and copies ran while one was open for 1% -> 0% of each run, Pallas kernels for 0% -> 0%
where the time goes in v1:
time: 123 us; the launch traced here: 122 us
  blocking collectives  94.7 us (77%)
  Pallas kernels  10.1 us (8%)
  starting transfers between devices  7.78 us (6%)
  local copies, waits for them, and re-layouts  6.32 us (5%)
  waiting for transfers between devices  3.07 us (2%)
    all_to_all x4, blocking collectives, exchange(): return lax.all_to_all(values, CHIPS, 0, 0)  94.7 us
    pallas_call x5, Pallas kernels, call(): pl.pallas_call(kernel, out_shape=out_shape, in_specs=[scalars] * smem + [...  10.1 us
    ppermute x2, starting transfers between devices, other_core(): return lax.ppermute(values, 'core', [(0, 1), (1, 0)])  7.78 us
    unnamed x34, local copies, waits for them, and re-layouts  6.32 us
    ppermute x2, waiting for transfers between devices, other_core(): return lax.ppermute(values, 'core', [(0, 1), (1, 0)])  3.07 us
  transfers between devices with their start and end apart: 2, of which 2 were waited for; matrix products, arithmetic and copies ran while one was open for 0% of the time, Pallas kernels for 0%

profile of v1, /device:TPU:1, one launch (start us, length us, event | category | flops | bytes accessed | tf_op | source)
XLA Modules:
  0.0 122.1 jit_solution(16696823090913368557)
XLA Ops:
  0.0 0.0 copy-start
  0.0 0.9 copy-done
  1.0 0.0 copy-start.2
  1.0 0.9 copy-done.2
  1.9 0.0 copy-start.4
  1.9 0.9 copy-done.4
  2.8 0.0 copy-start.6
  2.8 0.8 copy-done.6
  3.6 0.0 copy-start.9
  3.6 0.7 copy-done.9
  4.3 0.0 copy-start.11
  4.3 0.7 copy-done.11
  5.0 0.0 copy-start.13
  5.0 0.7 copy-done.13
  5.7 1.4 %shard_map.100 = (bf16[128,16,128]{2,1,0:T(8,128)(2,1)S(1)}, f32[1024,128]{1,0:T(8,128)S(1)}) custom-call(bf16[32,32,128]{2,1,0:T(8,128)(2,1)S(1)} %copy-done, s32[32,32]{1,0:T(8,128)S(1)} %copy-done.9, f32[2,128]{1,0:T(2,128)S(1)} %copy-done.11, f32[2,128]{1,0:T(2,128)S(1)} %copy-done.13, bf16[2,128,256]{2,1,0:T(8,128)(2,1)S(1)} %copy-done.2, ...), custom_call_target="tpu_custom_call" | custom-call | tf_op jit(solution)/shard_map/pallas_call | solution.py:185
  7.0 33.0 %all_to_all.20 = bf16[128,16,128]{2,1,0:T(8,128)(2,1)S(1)} all-to-all(bf16[128,16,128]{2,1,0:T(8,128)(2,1)S(1)} %get-tuple-element.10), channel_id=1, replica_groups=mesh['x'=4,'zh'=4,'zl'=2,'y'=4,'core'=2] {'x','zh','zl','y'}, dimensions={0} | all-to-all | bytes 1048576 | tf_op jit(solution)/shard_map/all_to_all | solution.py:200
  40.1 3.4 %collective-permute-start = (bf16[128,16,128]{2,1,0:T(8,128)(2,1)S(1)}, bf16[128,16,128]{2,1,0:T(8,128)(2,1)S(1)}, u32[]{:S(2)}, u32[]{:S(2)}) collective-permute-start(bf16[128,16,128]{2,1,0:T(8,128)(2,1)S(1)} %all_to_all.20), channel_id=1, source_target_pairs={{0,1},{1,0},{2,3},{3,2},{4,5},{5,4},{6,7},{7,6},{8,9},{9,8},{10,11... | collective-permute-start | bytes 1572872 | tf_op jit(solution)/shard_map/ppermute | solution.py:204
  43.5 1.5 %collective-permute-done = bf16[128,16,128]{2,1,0:T(8,128)(2,1)S(1)} collective-permute-done((bf16[128,16,128]{2,1,0:T(8,128)(2,1)S(1)}, bf16[128,16,128]{2,1,0:T(8,128)(2,1)S(1)}, u32[]{:S(2)}, u32[]{:S(2)}) %collective-permute-start) | collective-permute-done | bytes 524320 | tf_op jit(solution)/shard_map/ppermute | solution.py:204
  45.0 0.0 copy-start.7
  45.0 0.0 copy-start.8
  45.0 0.0 copy-start.10
  45.0 0.0 copy-start.14
  45.0 0.0 copy-start.15
  45.0 0.0 copy-start.16
  45.0 1.4 %shard_map.101 = bf16[16,8,8,128]{3,2,1,0:T(8,128)(2,1)S(1)} custom-call(s32[1]{0:T(128)} %bitcast.core, bf16[16,8,16,128]{3,2,1,0:T(8,128)(2,1)S(1)} %bitcast.7, bf16[16,8,16,128]{3,2,1,0:T(8,128)(2,1)S(1)} %bitcast.11), custom_call_target="tpu_custom_call" | custom-call | tf_op jit(solution)/shard_map/pallas_call | solution.py:185
  46.4 0.0 copy-start.1
  46.5 0.0 copy-start.3
  46.5 0.0 copy-start.5
  46.5 19.6 %all_to_all.21.y = bf16[128,8,128]{2,1,0:T(8,128)(2,1)S(1)} all-to-all(bf16[128,8,128]{2,1,0:T(8,128)(2,1)S(1)} %bitcast.10), channel_id=1, replica_groups=mesh['x'=4,'zh'=4,'zl'=2,'y'=4,'core'=2] {'x','zh','zl','y'}, dimensions={0} | all-to-all | bytes 524288 | tf_op jit(solution)/shard_map/all_to_all | solution.py:200
  66.0 0.0 copy-start.12
  66.0 0.0 copy-done.7
  66.1 0.0 copy-done.8
  66.1 0.0 copy-done.10
  66.1 0.0 copy-done.14
  66.1 0.0 copy-done.15
  66.1 0.0 copy-done.16
  66.1 0.0 copy-done.1
  66.1 0.0 copy-done.3
  66.1 0.0 copy-done.5
  66.1 0.6 copy-done.12
  66.7 4.7 %shard_map.102 = (bf16[128,16,128]{2,1,0:T(8,128)(2,1)S(1)}, f32[1024,128]{1,0:T(8,128)S(1)}, f32[1024,128]{1,0:T(8,128)S(1)}) custom-call(bf16[128,8,128]{2,1,0:T(8,128)(2,1)S(1)} %all_to_all.21.y, bf16[32,32,128]{2,1,0:T(8,128)(2,1)S(1)} %copy-done.1, f32[1024,128]{1,0:T(8,128)S(1)} %get-tuple-element.11.g_in, s32[32,32]{1,0:T(8,128)S(1)} %copy-done.10, ...), custom_call_target="tpu_custom_call" | custom-call | tf_op jit(solution)/shard_map/pallas_call | solution.py:185
  71.4 22.6 %all_to_all.22 = bf16[128,16,128]{2,1,0:T(8,128)(2,1)S(1)} all-to-all(bf16[128,16,128]{2,1,0:T(8,128)(2,1)S(1)} %get-tuple-element.12), channel_id=1, replica_groups=mesh['x'=4,'zh'=4,'zl'=2,'y'=4,'core'=2] {'x','zh','zl','y'}, dimensions={0} | all-to-all | bytes 1048576 | tf_op jit(solution)/shard_map/all_to_all | solution.py:200
  94.0 4.4 %collective-permute-start.1 = (bf16[128,16,128]{2,1,0:T(8,128)(2,1)S(1)}, bf16[128,16,128]{2,1,0:T(8,128)(2,1)S(1)}, u32[]{:S(2)}, u32[]{:S(2)}) collective-permute-start(bf16[128,16,128]{2,1,0:T(8,128)(2,1)S(1)} %all_to_all.22), channel_id=1, source_target_pairs={{0,1},{1,0},{2,3},{3,2},{4,5},{5,4},{6,7},{7,6},{8,9},{9,8},{10,11... | collective-permute-start | bytes 1572872 | tf_op jit(solution)/shard_map/ppermute | solution.py:204
  98.4 1.5 %collective-permute-done.1 = bf16[128,16,128]{2,1,0:T(8,128)(2,1)S(1)} collective-permute-done((bf16[128,16,128]{2,1,0:T(8,128)(2,1)S(1)}, bf16[128,16,128]{2,1,0:T(8,128)(2,1)S(1)}, u32[]{:S(2)}, u32[]{:S(2)}) %collective-permute-start.1) | collective-permute-done | bytes 524320 | tf_op jit(solution)/shard_map/ppermute | solution.py:204
  100.0 1.4 %shard_map.103 = bf16[8,2,8,8,128]{4,3,2,1,0:T(8,128)(2,1)S(1)} custom-call(s32[1]{0:T(128)} %bitcast.core, bf16[16,8,16,128]{3,2,1,0:T(8,128)(2,1)S(1)} %bitcast.8, bf16[16,8,16,128]{3,2,1,0:T(8,128)(2,1)S(1)} %bitcast.12), custom_call_target="tpu_custom_call" | custom-call | tf_op jit(solution)/shard_map/pallas_call | solution.py:185
  101.3 19.4 %all_to_all.23.y = bf16[128,8,128]{2,1,0:T(8,128)(2,1)S(1)} all-to-all(bf16[128,8,128]{2,1,0:T(8,128)(2,1)S(1)} %bitcast.9), channel_id=1, replica_groups=mesh['x'=4,'zh'=4,'zl'=2,'y'=4,'core'=2] {'x','zh','zl','y'}, dimensions={0} | all-to-all | bytes 524288 | tf_op jit(solution)/shard_map/all_to_all | solution.py:200
  120.8 1.3 %shard_map.104 = bf16[32,32,128]{2,1,0:T(8,128)(2,1)} custom-call(bf16[128,8,128]{2,1,0:T(8,128)(2,1)S(1)} %all_to_all.23.y, f32[1024,128]{1,0:T(8,128)S(1)} %get-tuple-element.13.z_in, f32[1024,128]{1,0:T(8,128)S(1)} %get-tuple-element.14.g_in, f32[2,128]{1,0:T(2,128)S(1)} %copy-done.15, f32[2,128]{1,0:T(2,128)S(1)} %copy-done.16, ...), custom_call_target="tpu_custom_call" | custom-call | tf_op jit(solution)/shard_map/pallas_call | solution.py:185
Async XLA Ops:
  0.0 0.9 copy-start
  1.0 0.9 copy-start.2
  1.9 0.9 copy-start.4
  2.8 0.8 copy-start.6
  3.6 0.7 copy-start.9
  4.3 0.7 copy-start.11
  5.0 0.7 copy-start.13
  40.1 4.9 %collective-permute-start = (bf16[128,16,128]{2,1,0:T(8,128)(2,1)S(1)}, bf16[128,16,128]{2,1,0:T(8,128)(2,1)S(1)}, u32[]{:S(2)}, u32[]{:S(2)}) collective-permute-start(bf16[128,16,128]{2,1,0:T(8,128)(2,1)S(1)} %all_to_all.20), channel_id=1, source_target_pairs={{0,1},{1,0},{2,3},{3,2},{4,5},{5,4},{6,7},{7,6},{8,9},{9,8},{10,11... | collective-permute-start | bytes 1572872 | tf_op jit(solution)/shard_map/ppermute | solution.py:204
  45.0 21.0 %copy-start.7 = (bf16[2,128,128]{2,1,0:T(8,128)(2,1)S(1)}, bf16[2,128,128]{2,1,0:T(8,128)(2,1)}, u32[]{:S(2)}) copy-start(bf16[2,128,128]{2,1,0:T(8,128)(2,1)} %out_gate.3) | copy-start | bytes 196612
  45.0 21.0 %copy-start.8 = (bf16[2,128,128]{2,1,0:T(8,128)(2,1)S(1)}, bf16[2,128,128]{2,1,0:T(8,128)(2,1)}, u32[]{:S(2)}) copy-start(bf16[2,128,128]{2,1,0:T(8,128)(2,1)} %out_weight.3) | copy-start | bytes 196612
  45.0 21.0 %copy-start.10 = (s32[32,32]{1,0:T(8,128)S(1)}, s32[32,32]{1,0:T(8,128)}, u32[]{:S(2)}) copy-start(s32[32,32]{1,0:T(8,128)} %mask.3) | copy-start | bytes 12292
  45.0 21.1 %copy-start.14 = (f32[2,128]{1,0:T(2,128)S(1)}, f32[2,128]{1,0:T(2,128)}, u32[]{:S(2)}) copy-start(f32[2,128]{1,0:T(2,128)} %in_bias.1) | copy-start | bytes 3076
  45.0 21.1 %copy-start.15 = (f32[2,128]{1,0:T(2,128)S(1)}, f32[2,128]{1,0:T(2,128)}, u32[]{:S(2)}) copy-start(f32[2,128]{1,0:T(2,128)} %out_gain.3) | copy-start | bytes 3076
  45.0 21.1 %copy-start.16 = (f32[2,128]{1,0:T(2,128)S(1)}, f32[2,128]{1,0:T(2,128)}, u32[]{:S(2)}) copy-start(f32[2,128]{1,0:T(2,128)} %out_bias.3) | copy-start | bytes 3076
  46.4 19.7 %copy-start.1 = (bf16[32,32,128]{2,1,0:T(8,128)(2,1)S(1)}, bf16[32,32,128]{2,1,0:T(8,128)(2,1)}, u32[]{:S(2)}) copy-start(bf16[32,32,128]{2,1,0:T(8,128)(2,1)} %pair.3) | copy-start | bytes 786436
  46.5 19.6 %copy-start.3 = (bf16[2,128,256]{2,1,0:T(8,128)(2,1)S(1)}, bf16[2,128,256]{2,1,0:T(8,128)(2,1)}, u32[]{:S(2)}) copy-start(bf16[2,128,256]{2,1,0:T(8,128)(2,1)} %weight.3) | copy-start | bytes 393220
  46.5 19.6 %copy-start.5 = (bf16[2,128,256]{2,1,0:T(8,128)(2,1)S(1)}, bf16[2,128,256]{2,1,0:T(8,128)(2,1)}, u32[]{:S(2)}) copy-start(bf16[2,128,256]{2,1,0:T(8,128)(2,1)} %gate.3) | copy-start | bytes 393220
  66.0 0.7 copy-start.12
  94.0 5.9 %collective-permute-start.1 = (bf16[128,16,128]{2,1,0:T(8,128)(2,1)S(1)}, bf16[128,16,128]{2,1,0:T(8,128)(2,1)S(1)}, u32[]{:S(2)}, u32[]{:S(2)}) collective-permute-start(bf16[128,16,128]{2,1,0:T(8,128)(2,1)S(1)} %all_to_all.22), channel_id=1, source_target_pairs={{0,1},{1,0},{2,3},{3,2},{4,5},{5,4},{6,7},{7,6},{8,9},{9,8},{10,11... | collective-permute-start | bytes 1572872 | tf_op jit(solution)/shard_map/ppermute | solution.py:204

commit v2 on v1

v2 whole, which is shorter than its diff:
```python
import jax
import jax.numpy as jnp
from jax import lax
from jax.experimental import pallas as pl
from jax.experimental.pallas import tpu as pltpu
from jax.sharding import Mesh
from jax.sharding import PartitionSpec as P

C = 128
T = 32
F32 = jnp.float32
BF16 = jnp.bfloat16
AXES = ("x1", "x0", "zh1", "zh0", "zl", "y1", "y0", "core")
CHIPS = AXES[:-1]
VMEM_LIMIT = 32 * 1024 * 1024


def dot(a, b):
    return jnp.dot(a, b, preferred_element_type=F32)


def dot_nt(a, b):
    return lax.dot_general(a, b, (((1,), (1,)), ((), ())), preferred_element_type=F32)


def sigmoid(v):
    return 0.5 * jnp.tanh(0.5 * v) + 0.5


def normalize(values, axis):
    average = jnp.mean(values, axis=axis, keepdims=True)
    centered = values - average
    variance = jnp.mean(centered * centered, axis=axis, keepdims=True)
    return centered * lax.rsqrt(variance + 1e-05)


def iota(shape, dim):
    return lax.broadcasted_iota(jnp.int32, shape, dim)


def group_select(rows):
    group = iota((8, C), 1) // T
    out = rows[0:8]
    for q in range(1, 4):
        out = jnp.where(group == q, rows[8 * q : 8 * q + 8], out)
    return out


def as_column(vector):
    return jnp.broadcast_to(vector, (C, C)).T


def swap_groups():
    src = iota((4 * C, 4 * C), 0)
    dst = iota((4 * C, 4 * C), 1)
    back = (dst & (T - 1)) | (((dst >> 5) & 3) << 7) | ((dst >> 7) << 5)
    return jnp.where(src == back, 1.0, 0.0).astype(BF16)


def emit_operands(projected, gate, mask_row, scratch, s):
    operands = sigmoid(gate) * projected * mask_row
    scratch[pl.ds(s, C, stride=16), :] = operands[:C]
    scratch[pl.ds(8 + s, C, stride=16), :] = operands[C:]


def first_kernel(
    pair_hbm, mask_hbm, gain_hbm, bias_hbm, weight_hbm, gate_hbm, lr,
    pair, mask, gain, bias, weight, gate, scratch, sems,
):
    moves = [
        (gain_hbm, gain), (bias_hbm, bias), (weight_hbm.at[0], weight), (gate_hbm.at[0], gate),
        (mask_hbm, mask), (pair_hbm, pair),
    ]
    copies = [pltpu.make_async_copy(a, b, sems.at[i]) for i, (a, b) in enumerate(moves)]
    for copy in copies:
        copy.start()
    for copy in copies:
        copy.wait()
    weight_t = weight[...].T
    gate_t = gate[...].T
    wide = jnp.where((iota((T, C), 1) & (T - 1)) == iota((T, C), 0), 1.0, 0.0).astype(BF16)
    mask_rows = group_select(dot(mask[...].astype(F32).astype(BF16), wide))
    for s in range(8):
        x = jnp.concatenate([pair[8 * q + s].astype(F32) for q in range(4)], axis=0)
        normed = (normalize(x, 1) * gain[0:1, :] + bias[0:1, :]).astype(BF16)
        emit_operands(
            dot_nt(weight_t, normed), dot_nt(gate_t, normed), mask_rows[s : s + 1], scratch, s
        )
    lr[...] = scratch[...].reshape(C, 16, C).astype(BF16)


def first_side_kernel(
    pair, mask, in_gain, in_bias, weight, gate, out_gate, out_gain, out_bias, out_weight,
    zt, gt, weight_t, out_weight_t, columns, mask_rows, scratch,
):
    scratch[...] = pair[...].astype(F32).reshape(T * T, C)
    out_gate_t = out_gate[0].T
    for s in range(8):
        z = jnp.concatenate([scratch[pl.ds(8 * q + s, T, stride=T), :] for q in range(4)], axis=0)
        normed = (normalize(z, 1) * in_gain[0:1, :] + in_bias[0:1, :]).astype(BF16)
        zt[s] = z.T
        gt[s] = sigmoid(dot_nt(out_gate_t, normed))
    weight_t[: 2 * C] = weight[1].T
    weight_t[2 * C :] = gate[1].T
    out_weight_t[...] = out_weight[0].T
    columns[0] = as_column(out_gain[0:1, :])
    columns[1] = as_column(out_bias[0:1, :])
    columns[2] = as_column(in_gain[1:2, :])
    columns[3] = as_column(in_bias[1:2, :])
    columns[4] = as_column(out_gain[1:2, :])
    columns[5] = as_column(out_bias[1:2, :])
    four = jnp.concatenate([mask[...].astype(F32).astype(BF16)] * 4, axis=0)
    eye = jnp.where(iota((T, T), 1) == iota((T, T), 0), 1.0, 0.0).astype(BF16)
    mask_rows[...] = group_select(dot_nt(eye, four))


def middle_kernel(
    y, zt, gt, weight_t, out_weight_t, columns, mask_rows, lr, z_out, scratch, scratch_y
):
    scratch_y[...] = y[...].astype(F32).reshape(8 * C, C)
    for s in range(8):
        product = scratch_y[pl.ds(s, C, stride=8), :]
        product = (normalize(product, 0) * columns[0] + columns[1]).astype(BF16)
        z = (zt[s] + gt[s] * dot(out_weight_t[...], product)).astype(BF16)
        z_out[s] = z
        normed = (normalize(z.astype(F32), 0) * columns[2] + columns[3]).astype(BF16)
        emit_operands(
            dot(weight_t[: 2 * C], normed), dot(weight_t[2 * C :], normed),
            mask_rows[s : s + 1], scratch, s,
        )
    lr[...] = scratch[...].reshape(C, 16, C).astype(BF16)


def second_side_kernel(zt, in_gain, in_bias, out_gate, z_out, g_out):
    for s in range(8):
        z = zt[s].astype(F32).T
        normed = (normalize(z, 1) * in_gain[1:2, :] + in_bias[1:2, :]).astype(BF16)
        opened = sigmoid(dot(normed, out_gate[1]))
        for q in range(4):
            rows = pl.ds(8 * q + s, T, stride=T)
            z_out[rows, :] = z[q * T : (q + 1) * T]
            g_out[rows, :] = opened[q * T : (q + 1) * T]


def last_kernel(y, z_in, g_in, columns, out_weight, out, scratch_y):
    scratch_y[...] = y[...].astype(F32).reshape(8 * C, C)
    for s in range(8):
        product = scratch_y[pl.ds(s, C, stride=8), :]
        product = normalize(product, 0) * columns[4] + columns[5]
        update = dot(product.T.astype(BF16), out_weight[1])
        for q in range(4):
            rows = pl.ds((8 * q + s) * T, T)
            piece = z_in[rows, :] + g_in[rows, :] * update[q * T : (q + 1) * T]
            out[8 * q + s] = piece.astype(BF16)


def outgoing_kernel(core, own, other, out, left, right):
    swap = swap_groups()
    half = core[0]
    for part, src in enumerate((own, other)):
        for quad in range(2):
            y = jnp.concatenate(
                [src[:, 4 * quad + c].reshape(256, C) for c in range(4)], axis=1
            )
            z = dot(y, swap).reshape(16, 16, 4 * C)
            depth = pl.ds((2 * part + quad) * C, C)
            for q in range(4):
                left[:, q, :, depth] = z[:, :8, q * C : (q + 1) * C]
                right[:, q, :, depth] = z[:, 8:, q * C : (q + 1) * C]
    a = left[...].reshape(512, 512).astype(BF16)
    pairs = right.reshape(8, 2, 4, 8, 512)
    b = jnp.concatenate([pairs[:, half, q].reshape(64, 512) for q in range(4)], axis=0)
    product = dot_nt(b.astype(BF16), a).astype(BF16)
    for quad in range(4):
        y = jnp.concatenate(
            [product[64 * q : 64 * q + 64, quad * C : (quad + 1) * C] for q in range(4)], axis=1
        )
        z = dot(y, swap)
        for r in range(4):
            out[4 * quad + r] = z[:, r * C : (r + 1) * C].reshape(8, 8, C).astype(BF16)


def incoming_kernel(core, own, other, out, left, right):
    swap = swap_groups()
    half = core[0]
    for part, src in enumerate((own, other)):
        for quad in range(4):
            y = jnp.concatenate([src[4 * quad + r].reshape(C, C) for r in range(4)], axis=1)
            z = dot(y, swap).reshape(8, 16, 4 * C)
            depth = pl.ds(quad * C, C)
            for q in range(4):
                left[q, part, :, :, depth] = z[:, :8, q * C : (q + 1) * C]
                if part == 0:
                    right[:, q, :, depth] = z[:, 8:, q * C : (q + 1) * C]
    a = left[...].reshape(512, 512).astype(BF16)
    b = right[...].reshape(256, 512).astype(BF16)
    product = dot_nt(a, b).astype(BF16)
    for quad in range(2):
        y = jnp.concatenate(
            [product[C * q : C * q + C, quad * C : (quad + 1) * C] for q in range(4)], axis=1
        )
        z = dot(y, swap)
        for c in range(4):
            piece = z[:, c * C : (c + 1) * C].reshape(2, 8, 8, C).astype(BF16)
            out[:, half, 4 * quad + c] = piece[0]
            out[:, 1 - half, 4 * quad + c] = piece[1]


def call(kernel, out_shape, scratch, *args, smem=0, hbm=False):
    vmem = pl.BlockSpec(memory_space=pltpu.VMEM)
    scalars = pl.BlockSpec(memory_space=pltpu.SMEM)
    space = pl.BlockSpec(memory_space=pltpu.HBM) if hbm else vmem
    if hbm:
        args = [pltpu.with_memory_space_constraint(arg, pltpu.HBM) for arg in args]
    return pl.pallas_call(
        kernel,
        out_shape=out_shape,
        in_specs=[scalars] * smem + [space] * (len(args) - smem),
        out_specs=[vmem] * len(out_shape) if isinstance(out_shape, list) else vmem,
        scratch_shapes=scratch,
        compiler_params=pltpu.CompilerParams(vmem_limit_bytes=VMEM_LIMIT),
    )(*args)


def struct(shape, dtype):
    return jax.ShapeDtypeStruct(shape, dtype)


def exchange(values):
    return lax.all_to_all(values, CHIPS, 0, 0)


def other_core(values):
    return lax.ppermute(values, "core", [(0, 1), (1, 0)])


def on_device(
    pair, pair_mask, in_gain, in_bias, weight, gate, out_gate, out_gain, out_bias, out_weight
):
    core = lax.axis_index("core").astype(jnp.int32).reshape(1)
    operands = struct((C, 16, C), BF16)
    slabs = struct((8, C, C), F32)
    rows = struct((T * T, C), F32)
    sides = [pltpu.VMEM((16, 4, 8, 512), F32), pltpu.VMEM((16, 4, 8, 512), F32)]

    lr = call(
        first_kernel, operands,
        [
            pltpu.VMEM((T, T, C), BF16), pltpu.VMEM((T, T), jnp.int32),
            pltpu.VMEM((2, C), F32), pltpu.VMEM((2, C), F32),
            pltpu.VMEM((C, 2 * C), BF16), pltpu.VMEM((C, 2 * C), BF16),
            pltpu.VMEM((16 * C, C), F32), pltpu.SemaphoreType.DMA((6,)),
        ],
        pair, pair_mask, in_gain, in_bias, weight, gate, hbm=True,
    )
    own, side_pair = lax.optimization_barrier((exchange(lr), pair))
    other = other_core(own)
    zt, gt, weight_t, out_weight_t, columns, mask_rows = call(
        first_side_kernel,
        [
            slabs, slabs, struct((4 * C, C), BF16), struct((C, C), BF16),
            struct((6, C, C), F32), struct((8, C), F32),
        ],
        [pltpu.VMEM((T * T, C), F32)],
        side_pair, pair_mask, in_gain, in_bias, weight, gate, out_gate, out_gain, out_bias,
        out_weight,
    )
    other, zt = lax.optimization_barrier((other, zt))
    y = call(
        outgoing_kernel, struct((16, 8, 8, C), BF16), sides,
        core, own.reshape(16, 8, 16, C), other.reshape(16, 8, 16, C), smem=1,
    )
    y = exchange(y.reshape(C, 8, C))
    lr, zt = call(
        middle_kernel, [operands, struct((8, C, C), BF16)],
        [pltpu.VMEM((16 * C, C), F32), pltpu.VMEM((8 * C, C), F32)],
        y, zt, gt, weight_t, out_weight_t, columns, mask_rows,
    )
    own, zt = lax.optimization_barrier((exchange(lr), zt))
    other = other_core(own)
    z, g = call(second_side_kernel, [rows, rows], [], zt, in_gain, in_bias, out_gate)
    other, z = lax.optimization_barrier((other, z))
    y = call(
        incoming_kernel, struct((8, 2, 8, 8, C), BF16),
        [pltpu.VMEM((4, 2, 8, 8, 512), F32), pltpu.VMEM((8, 4, 8, 512), F32)],
        core, own.reshape(16, 8, 16, C), other.reshape(16, 8, 16, C), smem=1,
    )
    y = exchange(y.reshape(C, 8, C))
    return call(
        last_kernel, struct((T, T, C), BF16), [pltpu.VMEM((8 * C, C), F32)],
        y, z, g, columns, out_weight,
    )


def solution(mesh):
    chips = Mesh(mesh.devices.reshape((2,) * 8), AXES)
    tile = P(AXES[:4], AXES[4:])
    return jax.shard_map(
        on_device,
        mesh=chips,
        in_specs=(tile, tile) + (P(),) * 8,
        out_specs=tile,
        check_vma=False,
    )
```

time: 123 us -> 115 us (0.935)
  local copies, waits for them, and re-layouts: 6.32 us -> 0.66 us
  waiting for transfers between devices: 3.07 us -> 0.24 us
    unnamed x34 -> x20, local copies, waits for them, and re-layouts: 6.32 us -> 0.66 us
    ppermute x2, waiting for transfers between devices: 3.07 us -> 0.24 us  [other_core(): return lax.ppermute(values, 'core', [(0, 1), (1, 0)])]
    pallas_call x5 -> x7, Pallas kernels: 10.1 us -> 11.3 us  [call(): pl.pallas_call(kernel, out_shape=out_shape, in_specs=[scalars] * smem + [...]
  transfers between devices with their start and end apart: 2 -> 2, of which waited for: 2 -> 1; matrix products, arithmetic and copies ran while one was open for 0% -> 0% of each run, Pallas kernels for 0% -> 2%
where the time goes in v2:
time: 115 us
  blocking collectives  95 us (83%)
  Pallas kernels  11.3 us (10%)
  starting transfers between devices  7.54 us (7%)
    all_to_all x4, blocking collectives, exchange(): return lax.all_to_all(values, CHIPS, 0, 0)  95 us
    pallas_call x7, Pallas kernels, call(): pl.pallas_call(kernel, out_shape=out_shape, in_specs=[scalars] * smem + [...  11.3 us
    ppermute x2, starting transfers between devices, other_core(): return lax.ppermute(values, 'core', [(0, 1), (1, 0)])  7.54 us
  transfers between devices with their start and end apart: 2, of which 1 were waited for; matrix products, arithmetic and copies ran while one was open for 0% of the time, Pallas kernels for 2%

profile of v2, /device:TPU:1, one launch (start us, length us, event | category | flops | bytes accessed | tf_op | source)
XLA Modules:
  0.0 115.0 jit_solution(3821886683936543074)
XLA Ops:
  0.0 2.4 %shard_map.100 = bf16[128,16,128]{2,1,0:T(8,128)(2,1)S(1)} custom-call(bf16[32,32,128]{2,1,0:T(8,128)(2,1)} %pair, s32[32,32]{1,0:T(8,128)} %mask.1, f32[2,128]{1,0:T(2,128)} %in_gain.3, f32[2,128]{1,0:T(2,128)} %in_bias.3, bf16[2,128,256]{2,1,0:T(8,128)(2,1)} %weight.1, bf16[2,128,256]{2,1,0:T(8,128)(2,1)} %gate.1), custom_call_target="tpu_custom_call" | custom-call | tf_op jit(solution)/shard_map/pallas_call | solution.py:215
  2.4 0.0 copy-start
  2.4 0.0 copy-start.1
  2.4 0.0 copy-start.2
  2.4 0.0 copy-start.3
  2.4 0.0 copy-start.4
  2.4 0.0 copy-start.5
  2.5 0.0 copy-start.7
  2.5 0.0 copy-start.8
  2.5 0.0 copy-start.9
  2.5 33.1 %all_to_all.20 = bf16[128,16,128]{2,1,0:T(8,128)(2,1)S(1)} all-to-all(bf16[128,16,128]{2,1,0:T(8,128)(2,1)S(1)} %shard_map.100), channel_id=1, replica_groups=mesh['x1'=2,'x0'=2,'zh1'=2,'zh0'=2,'zl'=2,'y1'=2,'y0'=2,'core'=2] {'x1',..., dimensions={0} | all-to-all | bytes 1048576 | tf_op jit(solution)/shard_map/all_to_all | solution.py:230
  35.6 3.5 %collective-permute-start = (bf16[128,16,128]{2,1,0:T(8,128)(2,1)S(1)}, bf16[128,16,128]{2,1,0:T(8,128)(2,1)S(1)}, u32[]{:S(2)}, u32[]{:S(2)}) collective-permute-start(bf16[128,16,128]{2,1,0:T(8,128)(2,1)S(1)} %all_to_all.20), channel_id=1, source_target_pairs={{0,1},{1,0},{2,3},{3,2},{4,5},{5,4},{6,7},{7,6},{8,9},{9,8},{10,11... | collective-permute-start | bytes 1572872 | tf_op jit(solution)/shard_map/ppermute | solution.py:234
  39.1 0.0 copy-start.6
  39.1 0.0 copy-done
  39.1 0.0 copy-done.1
  39.1 0.0 copy-done.2
  39.1 0.0 copy-done.3
  39.1 0.0 copy-done.4
  39.1 0.0 copy-done.5
  39.1 0.0 copy-done.7
  39.1 0.0 copy-done.8
  39.1 0.0 copy-done.9
  39.1 0.6 copy-done.6
  39.7 1.2 %shard_map.101 = (f32[8,128,128]{2,1,0:T(8,128)S(1)}, f32[8,128,128]{2,1,0:T(8,128)S(1)}, bf16[512,128]{1,0:T(8,128)(2,1)S(1)}, bf16[128,128]{1,0:T(8,128)(2,1)S...) custom-call(bf16[32,32,128]{2,1,0:T(8,128)(2,1)S(1)} %copy-done, s32[32,32]{1,0:T(8,128)S(1)} %copy-done.5, ...), custom_call_target="tpu_custom_call" | custom-call | tf_op jit(solution)/shard_map/pallas_call | solution.py:215
  40.9 0.0 collective-permute-done
  41.0 1.4 %shard_map.102 = bf16[16,8,8,128]{3,2,1,0:T(8,128)(2,1)S(1)} custom-call(s32[1]{0:T(128)} %bitcast.core, bf16[16,8,16,128]{3,2,1,0:T(8,128)(2,1)S(1)} %bitcast.7, bf16[16,8,16,128]{3,2,1,0:T(8,128)(2,1)S(1)} %bitcast.11), custom_call_target="tpu_custom_call" | custom-call | tf_op jit(solution)/shard_map/pallas_call | solution.py:215
  42.4 19.9 %all_to_all.21.y = bf16[128,8,128]{2,1,0:T(8,128)(2,1)S(1)} all-to-all(bf16[128,8,128]{2,1,0:T(8,128)(2,1)S(1)} %bitcast.10), channel_id=1, replica_groups=mesh['x1'=2,'x0'=2,'zh1'=2,'zh0'=2,'zl'=2,'y1'=2,'y0'=2,'core'=2] {'x1',..., dimensions={0} | all-to-all | bytes 524288 | tf_op jit(solution)/shard_map/all_to_all | solution.py:230
  62.2 2.5 %shard_map.103 = (bf16[128,16,128]{2,1,0:T(8,128)(2,1)S(1)}, bf16[8,128,128]{2,1,0:T(8,128)(2,1)S(1)}) custom-call(bf16[128,8,128]{2,1,0:T(8,128)(2,1)S(1)} %all_to_all.21.y, f32[8,128,128]{2,1,0:T(8,128)S(1)} %get-tuple-element.27.zt, f32[8,128,128]{2,1,0:T(8,128)S(1)} %get-tuple-element.28.gt, bf16[512,128]{1,0:T(8,128)(2,1)S(1)} %get-tuple-element.29.weight_t, ...), custom_call_target="tpu_custom_call" | custom-call | tf_op jit(solution)/shard_map/pallas_call | solution.py:215
  64.8 22.6 %all_to_all.22 = bf16[128,16,128]{2,1,0:T(8,128)(2,1)S(1)} all-to-all(bf16[128,16,128]{2,1,0:T(8,128)(2,1)S(1)} %get-tuple-element.33), channel_id=1, replica_groups=mesh['x1'=2,'x0'=2,'zh1'=2,'zh0'=2,'zl'=2,'y1'=2,'y0'=2,'core'=2] {'x1',..., dimensions={0} | all-to-all | bytes 1048576 | tf_op jit(solution)/shard_map/all_to_all | solution.py:230
  87.4 4.1 %collective-permute-start.1 = (bf16[128,16,128]{2,1,0:T(8,128)(2,1)S(1)}, bf16[128,16,128]{2,1,0:T(8,128)(2,1)S(1)}, u32[]{:S(2)}, u32[]{:S(2)}) collective-permute-start(bf16[128,16,128]{2,1,0:T(8,128)(2,1)S(1)} %all_to_all.22), channel_id=1, source_target_pairs={{0,1},{1,0},{2,3},{3,2},{4,5},{5,4},{6,7},{7,6},{8,9},{9,8},{10,11... | collective-permute-start | bytes 1572872 | tf_op jit(solution)/shard_map/ppermute | solution.py:234
  91.4 1.3 %shard_map.104 = (f32[1024,128]{1,0:T(8,128)S(1)}, f32[1024,128]{1,0:T(8,128)S(1)}) custom-call(bf16[8,128,128]{2,1,0:T(8,128)(2,1)S(1)} %get-tuple-element.36.zt, f32[2,128]{1,0:T(2,128)S(1)} %copy-done.6, f32[2,128]{1,0:T(2,128)S(1)} %copy-done.7, bf16[2,128,128]{2,1,0:T(8,128)(2,1)S(1)} %copy-done.3), custom_call_target="tpu_custom_call" | custom-call | tf_op jit(solution)/shard_map/pallas_call | solution.py:215
  92.7 0.2 collective-permute-done.1
  93.0 1.4 %shard_map.105 = bf16[8,2,8,8,128]{4,3,2,1,0:T(8,128)(2,1)S(1)} custom-call(s32[1]{0:T(128)} %bitcast.core, bf16[16,8,16,128]{3,2,1,0:T(8,128)(2,1)S(1)} %bitcast.8, bf16[16,8,16,128]{3,2,1,0:T(8,128)(2,1)S(1)} %bitcast.12), custom_call_target="tpu_custom_call" | custom-call | tf_op jit(solution)/shard_map/pallas_call | solution.py:215
  94.4 19.5 %all_to_all.23.y = bf16[128,8,128]{2,1,0:T(8,128)(2,1)S(1)} all-to-all(bf16[128,8,128]{2,1,0:T(8,128)(2,1)S(1)} %bitcast.9), channel_id=1, replica_groups=mesh['x1'=2,'x0'=2,'zh1'=2,'zh0'=2,'zl'=2,'y1'=2,'y0'=2,'core'=2] {'x1',..., dimensions={0} | all-to-all | bytes 524288 | tf_op jit(solution)/shard_map/all_to_all | solution.py:230
  113.8 1.2 %shard_map.106 = bf16[32,32,128]{2,1,0:T(8,128)(2,1)} custom-call(bf16[128,8,128]{2,1,0:T(8,128)(2,1)S(1)} %all_to_all.23.y, f32[1024,128]{1,0:T(8,128)S(1)} %get-tuple-element.39.z_in, f32[1024,128]{1,0:T(8,128)S(1)} %get-tuple-element.40.g_in, f32[6,128,128]{2,1,0:T(8,128)S(1)} %get-tuple-element.31.columns, bf16[2,128,128]{2,1,0:T(8,128)(2,1)S(1)} %copy-done.4), custom_call_target="tpu_custom_call" | custom-call | tf_op jit(solution)/shard_map/pallas_call | solution.py:215
Async XLA Ops:
  2.4 36.7 %copy-start = (bf16[32,32,128]{2,1,0:T(8,128)(2,1)S(1)}, bf16[32,32,128]{2,1,0:T(8,128)(2,1)}, u32[]{:S(2)}) copy-start(bf16[32,32,128]{2,1,0:T(8,128)(2,1)} %pair) | copy-start | bytes 786436
  2.4 36.7 %copy-start.1 = (bf16[2,128,256]{2,1,0:T(8,128)(2,1)S(1)}, bf16[2,128,256]{2,1,0:T(8,128)(2,1)}, u32[]{:S(2)}) copy-start(bf16[2,128,256]{2,1,0:T(8,128)(2,1)} %weight.1) | copy-start | bytes 393220
  2.4 36.7 %copy-start.2 = (bf16[2,128,256]{2,1,0:T(8,128)(2,1)S(1)}, bf16[2,128,256]{2,1,0:T(8,128)(2,1)}, u32[]{:S(2)}) copy-start(bf16[2,128,256]{2,1,0:T(8,128)(2,1)} %gate.1) | copy-start | bytes 393220
  2.4 36.7 %copy-start.3 = (bf16[2,128,128]{2,1,0:T(8,128)(2,1)S(1)}, bf16[2,128,128]{2,1,0:T(8,128)(2,1)}, u32[]{:S(2)}) copy-start(bf16[2,128,128]{2,1,0:T(8,128)(2,1)} %out_gate.3) | copy-start | bytes 196612
  2.4 36.7 %copy-start.4 = (bf16[2,128,128]{2,1,0:T(8,128)(2,1)S(1)}, bf16[2,128,128]{2,1,0:T(8,128)(2,1)}, u32[]{:S(2)}) copy-start(bf16[2,128,128]{2,1,0:T(8,128)(2,1)} %out_weight.3) | copy-start | bytes 196612
  2.4 36.7 %copy-start.5 = (s32[32,32]{1,0:T(8,128)S(1)}, s32[32,32]{1,0:T(8,128)}, u32[]{:S(2)}) copy-start(s32[32,32]{1,0:T(8,128)} %mask.1) | copy-start | bytes 12292
  2.5 36.7 %copy-start.7 = (f32[2,128]{1,0:T(2,128)S(1)}, f32[2,128]{1,0:T(2,128)}, u32[]{:S(2)}) copy-start(f32[2,128]{1,0:T(2,128)} %in_bias.3) | copy-start | bytes 3076
  2.5 36.7 %copy-start.8 = (f32[2,128]{1,0:T(2,128)S(1)}, f32[2,128]{1,0:T(2,128)}, u32[]{:S(2)}) copy-start(f32[2,128]{1,0:T(2,128)} %out_gain.1) | copy-start | bytes 3076
  2.5 36.7 %copy-start.9 = (f32[2,128]{1,0:T(2,128)S(1)}, f32[2,128]{1,0:T(2,128)}, u32[]{:S(2)}) copy-start(f32[2,128]{1,0:T(2,128)} %out_bias.1) | copy-start | bytes 3076
  35.6 5.3 %collective-permute-start = (bf16[128,16,128]{2,1,0:T(8,128)(2,1)S(1)}, bf16[128,16,128]{2,1,0:T(8,128)(2,1)S(1)}, u32[]{:S(2)}, u32[]{:S(2)}) collective-permute-start(bf16[128,16,128]{2,1,0:T(8,128)(2,1)S(1)} %all_to_all.20), channel_id=1, source_target_pairs={{0,1},{1,0},{2,3},{3,2},{4,5},{5,4},{6,7},{7,6},{8,9},{9,8},{10,11... | collective-permute-start | bytes 1572872 | tf_op jit(solution)/shard_map/ppermute | solution.py:234
  39.1 0.7 copy-start.6
  87.4 5.6 %collective-permute-start.1 = (bf16[128,16,128]{2,1,0:T(8,128)(2,1)S(1)}, bf16[128,16,128]{2,1,0:T(8,128)(2,1)S(1)}, u32[]{:S(2)}, u32[]{:S(2)}) collective-permute-start(bf16[128,16,128]{2,1,0:T(8,128)(2,1)S(1)} %all_to_all.22), channel_id=1, source_target_pairs={{0,1},{1,0},{2,3},{3,2},{4,5},{5,4},{6,7},{7,6},{8,9},{9,8},{10,11... | collective-permute-start | bytes 1572872 | tf_op jit(solution)/shard_map/ppermute | solution.py:234

commit v3 on v2

--- a/solution.py
+++ b/solution.py
@@ -11,8 +11,27 @@
 F32 = jnp.float32
 BF16 = jnp.bfloat16
 AXES = ("x1", "x0", "zh1", "zh0", "zl", "y1", "y0", "core")
-CHIPS = AXES[:-1]
+FIRST = (2, 5, 2)
+
+
+def away(place):
+    x, z, y = place >> 5, (place >> 2) & 7, place & 3
+    return (x - FIRST[0]) % 4, (z - FIRST[1]) % 8, (y - FIRST[2]) % 4
+
+
+def hops(place):
+    x, z, y = away(place)
+    return min(x, 4 - x) + min(z, 8 - z) + min(y, 4 - y)
+
+
+PLACES = sorted(range(C), key=lambda place: (hops(place) > 0, -hops(place), away(place)))
+RANKS = {place: i for i, place in enumerate(PLACES)}
+GROUPS = [[2 * place + core for place in PLACES] for core in range(2)]
 VMEM_LIMIT = 32 * 1024 * 1024
+
+
+def rank(row, pair_col):
+    return RANKS[8 * row + pair_col]
 
 
 def dot(a, b):
@@ -57,10 +76,12 @@
     return jnp.where(src == back, 1.0, 0.0).astype(BF16)
 
 
-def emit_operands(projected, gate, mask_row, scratch, s):
-    operands = sigmoid(gate) * projected * mask_row
-    scratch[pl.ds(s, C, stride=16), :] = operands[:C]
-    scratch[pl.ds(8 + s, C, stride=16), :] = operands[C:]
+def emit_operands(multiply, weight_t, gate_t, normed, mask_rows, scratch, s):
+    masks = jnp.concatenate([mask_rows[s : s + 1], mask_rows[s + 1 : s + 2]], axis=1)
+    operands = sigmoid(multiply(gate_t, normed)) * multiply(weight_t, normed) * masks
+    for i in range(2):
+        scratch[pl.ds(s + i, C, stride=16), :] = operands[:C, i * C : (i + 1) * C]
+        scratch[pl.ds(8 + s + i, C, stride=16), :] = operands[C:, i * C : (i + 1) * C]
 
 
 def first_kernel(
@@ -68,24 +89,27 @@
     pair, mask, gain, bias, weight, gate, scratch, sems,
 ):
     moves = [
-        (gain_hbm, gain), (bias_hbm, bias), (weight_hbm.at[0], weight), (gate_hbm.at[0], gate),
-        (mask_hbm, mask), (pair_hbm, pair),
+        (weight_hbm.at[0], weight), (gate_hbm.at[0], gate), (mask_hbm, mask),
+        (gain_hbm, gain), (bias_hbm, bias), (pair_hbm, pair),
     ]
     copies = [pltpu.make_async_copy(a, b, sems.at[i]) for i, (a, b) in enumerate(moves)]
     for copy in copies:
         copy.start()
-    for copy in copies:
+    wide = jnp.where((iota((T, C), 1) & (T - 1)) == iota((T, C), 0), 1.0, 0.0).astype(BF16)
+    for copy in copies[:3]:
         copy.wait()
     weight_t = weight[...].T
     gate_t = gate[...].T
-    wide = jnp.where((iota((T, C), 1) & (T - 1)) == iota((T, C), 0), 1.0, 0.0).astype(BF16)
     mask_rows = group_select(dot(mask[...].astype(F32).astype(BF16), wide))
-    for s in range(8):
-        x = jnp.concatenate([pair[8 * q + s].astype(F32) for q in range(4)], axis=0)
-        normed = (normalize(x, 1) * gain[0:1, :] + bias[0:1, :]).astype(BF16)
-        emit_operands(
-            dot_nt(weight_t, normed), dot_nt(gate_t, normed), mask_rows[s : s + 1], scratch, s
-        )
+    for copy in copies[3:]:
+        copy.wait()
+    normed = []
+    for s in range(0, 8, 2):
+        tokens = [pair[8 * q + s + i].astype(F32) for i in range(2) for q in range(4)]
+        x = normalize(jnp.concatenate(tokens, axis=0), 1)
+        normed.append((x * gain[0:1, :] + bias[0:1, :]).astype(BF16))
+    for s in range(0, 8, 2):
+        emit_operands(dot_nt, weight_t, gate_t, normed[s // 2], mask_rows, scratch, s)
     lr[...] = scratch[...].reshape(C, 16, C).astype(BF16)
 
 
@@ -118,15 +142,22 @@
     y, zt, gt, weight_t, out_weight_t, columns, mask_rows, lr, z_out, scratch, scratch_y
 ):
     scratch_y[...] = y[...].astype(F32).reshape(8 * C, C)
-    for s in range(8):
-        product = scratch_y[pl.ds(s, C, stride=8), :]
-        product = (normalize(product, 0) * columns[0] + columns[1]).astype(BF16)
-        z = (zt[s] + gt[s] * dot(out_weight_t[...], product)).astype(BF16)
-        z_out[s] = z
-        normed = (normalize(z.astype(F32), 0) * columns[2] + columns[3]).astype(BF16)
+    twice = [jnp.concatenate([columns[i], columns[i]], axis=1) for i in range(4)]
+    normed = []
+    for s in range(0, 8, 2):
+        slabs = [scratch_y[pl.ds(s + i, C, stride=8), :] for i in range(2)]
+        product = normalize(jnp.concatenate(slabs, axis=1), 0)
+        product = (product * twice[0] + twice[1]).astype(BF16)
+        update = dot(out_weight_t[...], product)
+        z = jnp.concatenate([zt[s], zt[s + 1]], axis=1)
+        g = jnp.concatenate([gt[s], gt[s + 1]], axis=1)
+        z = (z + g * update).astype(BF16)
+        z_out[s] = z[:, :C]
+        z_out[s + 1] = z[:, C:]
+        normed.append((normalize(z.astype(F32), 0) * twice[2] + twice[3]).astype(BF16))
+    for s in range(0, 8, 2):
         emit_operands(
-            dot(weight_t[: 2 * C], normed), dot(weight_t[2 * C :], normed),
-            mask_rows[s : s + 1], scratch, s,
+            dot, weight_t[: 2 * C], weight_t[2 * C :], normed[s // 2], mask_rows[...], scratch, s
         )
     lr[...] = scratch[...].reshape(C, 16, C).astype(BF16)
 
@@ -160,7 +191,11 @@
     for part, src in enumerate((own, other)):
         for quad in range(2):
             y = jnp.concatenate(
-                [src[:, 4 * quad + c].reshape(256, C) for c in range(4)], axis=1
+                [
+                    jnp.concatenate([src[rank(r, 4 * quad + c)] for r in range(16)], axis=0)
+                    for c in range(4)
+                ],
+                axis=1,
             )
             z = dot(y, swap).reshape(16, 16, 4 * C)
             depth = pl.ds((2 * part + quad) * C, C)
@@ -177,7 +212,9 @@
         )
         z = dot(y, swap)
         for r in range(4):
-            out[4 * quad + r] = z[:, r * C : (r + 1) * C].reshape(8, 8, C).astype(BF16)
+            piece = z[:, r * C : (r + 1) * C].reshape(8, 8, C).astype(BF16)
+            for c in range(8):
+                out[rank(4 * quad + r, c)] = piece[c]
 
 
 def incoming_kernel(core, own, other, out, left, right):
@@ -185,7 +222,13 @@
     half = core[0]
     for part, src in enumerate((own, other)):
         for quad in range(4):
-            y = jnp.concatenate([src[4 * quad + r].reshape(C, C) for r in range(4)], axis=1)
+            y = jnp.concatenate(
+                [
+                    jnp.concatenate([src[rank(4 * quad + r, c)] for c in range(8)], axis=0)
+                    for r in range(4)
+                ],
+                axis=1,
+            )
             z = dot(y, swap).reshape(8, 16, 4 * C)
             depth = pl.ds(quad * C, C)
             for q in range(4):
@@ -202,8 +245,10 @@
         z = dot(y, swap)
         for c in range(4):
             piece = z[:, c * C : (c + 1) * C].reshape(2, 8, 8, C).astype(BF16)
-            out[:, half, 4 * quad + c] = piece[0]
-            out[:, 1 - half, 4 * quad + c] = piece[1]
+            for r in range(8):
+                even, odd = rank(2 * r, 4 * quad + c), rank(2 * r + 1, 4 * quad + c)
+                out[even + (odd - even) * half] = piece[0, r]
+                out[odd - (odd - even) * half] = piece[1, r]
 
 
 def call(kernel, out_shape, scratch, *args, smem=0, hbm=False):
@@ -227,7 +272,7 @@
 
 
 def exchange(values):
-    return lax.all_to_all(values, CHIPS, 0, 0)
+    return lax.all_to_all(values, AXES, 0, 0, axis_index_groups=GROUPS)
 
 
 def other_core(values):
@@ -267,10 +312,10 @@
     )
     other, zt = lax.optimization_barrier((other, zt))
     y = call(
-        outgoing_kernel, struct((16, 8, 8, C), BF16), sides,
-        core, own.reshape(16, 8, 16, C), other.reshape(16, 8, 16, C), smem=1,
-    )
-    y = exchange(y.reshape(C, 8, C))
+        outgoing_kernel, struct((C, 8, C), BF16), sides,
+        core, own, other, smem=1,
+    )
+    y = exchange(y)
     lr, zt = call(
         middle_kernel, [operands, struct((8, C, C), BF16)],
         [pltpu.VMEM((16 * C, C), F32), pltpu.VMEM((8 * C, C), F32)],
@@ -281,11 +326,11 @@
     z, g = call(second_side_kernel, [rows, rows], [], zt, in_gain, in_bias, out_gate)
     other, z = lax.optimization_barrier((other, z))
     y = call(
-        incoming_kernel, struct((8, 2, 8, 8, C), BF16),
+        incoming_kernel, struct((C, 8, C), BF16),
         [pltpu.VMEM((4, 2, 8, 8, 512), F32), pltpu.VMEM((8, 4, 8, 512), F32)],
-        core, own.reshape(16, 8, 16, C), other.reshape(16, 8, 16, C), smem=1,
-    )
-    y = exchange(y.reshape(C, 8, C))
+        core, own, other, smem=1,
+    )
+    y = exchange(y)
     return call(
         last_kernel, struct((T, T, C), BF16), [pltpu.VMEM((8 * C, C), F32)],
         y, z, g, columns, out_weight,

time: 115 us -> 107 us (0.930)
  starting transfers between devices: 7.54 us -> 2.64 us
  Pallas kernels: 11.3 us -> 9.58 us
  blocking collectives: 95 us -> 93.4 us
    ppermute x2, starting transfers between devices: 7.54 us -> 2.64 us  [other_core(): return lax.ppermute(values, 'core', [(0, 1), (1, 0)])]
    pallas_call x7, Pallas kernels: 11.3 us -> 9.58 us  [call(): pl.pallas_call(kernel, out_shape=out_shape, in_specs=[scalars] * smem + [...]
    all_to_all x4, blocking collectives: 95 us -> 93.4 us  [exchange(): return lax.all_to_all(values, AXES, 0, 0, axis_index_groups=GROUPS)]
where the time goes in v3:
time: 107 us
  blocking collectives  93.4 us (87%)
  Pallas kernels  9.58 us (9%)
  starting transfers between devices  2.64 us (2%)
    all_to_all x4, blocking collectives, exchange(): return lax.all_to_all(values, AXES, 0, 0, axis_index_groups=GROUPS)  93.4 us
    pallas_call x7, Pallas kernels, call(): pl.pallas_call(kernel, out_shape=out_shape, in_specs=[scalars] * smem + [...  9.58 us
    ppermute x2, starting transfers between devices, other_core(): return lax.ppermute(values, 'core', [(0, 1), (1, 0)])  2.64 us
  transfers between devices with their start and end apart: 2, of which 1 were waited for; matrix products, arithmetic and copies ran while one was open for 0% of the time, Pallas kernels for 2%

profile of v3, /device:TPU:1, one launch (start us, length us, event | category | flops | bytes accessed | tf_op | source)
XLA Modules:
  0.0 106.7 jit_solution(8224257358985580364)
XLA Ops:
  0.0 2.1 %shard_map.100 = bf16[128,16,128]{2,1,0:T(8,128)(2,1)S(1)} custom-call(bf16[32,32,128]{2,1,0:T(8,128)(2,1)} %pair, s32[32,32]{1,0:T(8,128)} %mask.1, f32[2,128]{1,0:T(2,128)} %in_gain.3, f32[2,128]{1,0:T(2,128)} %in_bias.3, bf16[2,128,256]{2,1,0:T(8,128)(2,1)} %weight.1, bf16[2,128,256]{2,1,0:T(8,128)(2,1)} %gate.1), custom_call_target="tpu_custom_call" | custom-call | tf_op jit(solution)/shard_map/pallas_call | solution.py:260
  2.1 0.0 copy-start
  2.1 0.0 copy-start.1
  2.1 0.0 copy-start.2
  2.1 0.0 copy-start.3
  2.2 0.0 copy-start.4
  2.2 0.0 copy-start.5
  2.2 0.0 copy-start.7
  2.2 0.0 copy-start.8
  2.2 0.0 copy-start.9
  2.2 29.4 %all_to_all.20.own = bf16[128,16,128]{2,1,0:T(8,128)(2,1)S(1)} all-to-all(bf16[128,16,128]{2,1,0:T(8,128)(2,1)S(1)} %shard_map.100), channel_id=1, replica_groups={{172,8,200,0,14,10,16,72,136,192,206,202,208,56,6,2,12,22,18,24,64,78,7..., dimensions={0} | all-to-all | bytes 1048576 | tf_op jit(solution)/shard_map/all_to_all | solution.py:275
  31.6 1.1 %collective-permute-start = (bf16[128,16,128]{2,1,0:T(8,128)(2,1)S(1)}, bf16[128,16,128]{2,1,0:T(8,128)(2,1)S(1)}, u32[]{:S(2)}, u32[]{:S(2)}) collective-permute-start(bf16[128,16,128]{2,1,0:T(8,128)(2,1)S(1)} %all_to_all.20.own), channel_id=1, source_target_pairs={{0,1},{1,0},{2,3},{3,2},{4,5},{5,4},{6,7},{7,6},{8,9},{9,8},{10,11... | collective-permute-start | bytes 1572872 | tf_op jit(solution)/shard_map/ppermute | solution.py:279
  32.8 0.0 copy-start.6
  32.8 0.0 copy-done
  32.8 0.0 copy-done.1
  32.8 0.0 copy-done.2
  32.8 0.0 copy-done.3
  32.8 0.0 copy-done.4
  32.8 0.0 copy-done.5
  32.8 0.0 copy-done.7
  32.8 0.0 copy-done.8
  32.8 0.0 copy-done.9
  32.8 0.6 copy-done.6
  33.4 1.2 %shard_map.101 = (f32[8,128,128]{2,1,0:T(8,128)S(1)}, f32[8,128,128]{2,1,0:T(8,128)S(1)}, bf16[512,128]{1,0:T(8,128)(2,1)S(1)}, bf16[128,128]{1,0:T(8,128)(2,1)S...) custom-call(bf16[32,32,128]{2,1,0:T(8,128)(2,1)S(1)} %copy-done, s32[32,32]{1,0:T(8,128)S(1)} %copy-done.5, ...), custom_call_target="tpu_custom_call" | custom-call | tf_op jit(solution)/shard_map/pallas_call | solution.py:260
  34.6 0.0 collective-permute-done.other
  34.7 1.4 %shard_map.102 = bf16[128,8,128]{2,1,0:T(8,128)(2,1)S(1)} custom-call(s32[1]{0:T(128)} %bitcast.core, bf16[128,16,128]{2,1,0:T(8,128)(2,1)S(1)} %all_to_all.20.own, bf16[128,16,128]{2,1,0:T(8,128)(2,1)S(1)} %collective-permute-done.other), custom_call_target="tpu_custom_call" | custom-call | tf_op jit(solution)/shard_map/pallas_call | solution.py:260
  36.1 19.6 %all_to_all.21.y = bf16[128,8,128]{2,1,0:T(8,128)(2,1)S(1)} all-to-all(bf16[128,8,128]{2,1,0:T(8,128)(2,1)S(1)} %shard_map.102), channel_id=1, replica_groups={{172,8,200,0,14,10,16,72,136,192,206,202,208,56,6,2,12,22,18,24,64,78,7..., dimensions={0} | all-to-all | bytes 524288 | tf_op jit(solution)/shard_map/all_to_all | solution.py:275
  55.7 1.0 shard_map.103
  56.7 24.9 %all_to_all.22.own = bf16[128,16,128]{2,1,0:T(8,128)(2,1)S(1)} all-to-all(bf16[128,16,128]{2,1,0:T(8,128)(2,1)S(1)} %get-tuple-element.33), channel_id=1, replica_groups={{172,8,200,0,14,10,16,72,136,192,206,202,208,56,6,2,12,22,18,24,64,78,7..., dimensions={0} | all-to-all | bytes 1048576 | tf_op jit(solution)/shard_map/all_to_all | solution.py:275
  81.6 1.5 %collective-permute-start.1 = (bf16[128,16,128]{2,1,0:T(8,128)(2,1)S(1)}, bf16[128,16,128]{2,1,0:T(8,128)(2,1)S(1)}, u32[]{:S(2)}, u32[]{:S(2)}) collective-permute-start(bf16[128,16,128]{2,1,0:T(8,128)(2,1)S(1)} %all_to_all.22.own), channel_id=1, source_target_pairs={{0,1},{1,0},{2,3},{3,2},{4,5},{5,4},{6,7},{7,6},{8,9},{9,8},{10,11... | collective-permute-start | bytes 1572872 | tf_op jit(solution)/shard_map/ppermute | solution.py:279
  83.1 1.3 %shard_map.104 = (f32[1024,128]{1,0:T(8,128)S(1)}, f32[1024,128]{1,0:T(8,128)S(1)}) custom-call(bf16[8,128,128]{2,1,0:T(8,128)(2,1)S(1)} %get-tuple-element.36.zt, f32[2,128]{1,0:T(2,128)S(1)} %copy-done.6, f32[2,128]{1,0:T(2,128)S(1)} %copy-done.7, bf16[2,128,128]{2,1,0:T(8,128)(2,1)S(1)} %copy-done.3), custom_call_target="tpu_custom_call" | custom-call | tf_op jit(solution)/shard_map/pallas_call | solution.py:260
  84.4 0.2 collective-permute-done.1.other
  84.6 1.4 %shard_map.105 = bf16[128,8,128]{2,1,0:T(8,128)(2,1)S(1)} custom-call(s32[1]{0:T(128)} %bitcast.core, bf16[128,16,128]{2,1,0:T(8,128)(2,1)S(1)} %all_to_all.22.own, bf16[128,16,128]{2,1,0:T(8,128)(2,1)S(1)} %collective-permute-done.1.other), custom_call_target="tpu_custom_call" | custom-call | tf_op jit(solution)/shard_map/pallas_call | solution.py:260
  86.0 19.5 %all_to_all.23.y = bf16[128,8,128]{2,1,0:T(8,128)(2,1)S(1)} all-to-all(bf16[128,8,128]{2,1,0:T(8,128)(2,1)S(1)} %shard_map.105), channel_id=1, replica_groups={{172,8,200,0,14,10,16,72,136,192,206,202,208,56,6,2,12,22,18,24,64,78,7..., dimensions={0} | all-to-all | bytes 524288 | tf_op jit(solution)/shard_map/all_to_all | solution.py:275
  105.5 1.2 %shard_map.106 = bf16[32,32,128]{2,1,0:T(8,128)(2,1)} custom-call(bf16[128,8,128]{2,1,0:T(8,128)(2,1)S(1)} %all_to_all.23.y, f32[1024,128]{1,0:T(8,128)S(1)} %get-tuple-element.39.z_in, f32[1024,128]{1,0:T(8,128)S(1)} %get-tuple-element.40.g_in, f32[6,128,128]{2,1,0:T(8,128)S(1)} %get-tuple-element.31.columns, bf16[2,128,128]{2,1,0:T(8,128)(2,1)S(1)} %copy-done.4), custom_call_target="tpu_custom_call" | custom-call | tf_op jit(solution)/shard_map/pallas_call | solution.py:260
Async XLA Ops:
  2.1 30.7 %copy-start = (bf16[32,32,128]{2,1,0:T(8,128)(2,1)S(1)}, bf16[32,32,128]{2,1,0:T(8,128)(2,1)}, u32[]{:S(2)}) copy-start(bf16[32,32,128]{2,1,0:T(8,128)(2,1)} %pair) | copy-start | bytes 786436
  2.1 30.6 %copy-start.1 = (bf16[2,128,256]{2,1,0:T(8,128)(2,1)S(1)}, bf16[2,128,256]{2,1,0:T(8,128)(2,1)}, u32[]{:S(2)}) copy-start(bf16[2,128,256]{2,1,0:T(8,128)(2,1)} %weight.1) | copy-start | bytes 393220
  2.1 30.6 %copy-start.2 = (bf16[2,128,256]{2,1,0:T(8,128)(2,1)S(1)}, bf16[2,128,256]{2,1,0:T(8,128)(2,1)}, u32[]{:S(2)}) copy-start(bf16[2,128,256]{2,1,0:T(8,128)(2,1)} %gate.1) | copy-start | bytes 393220
  2.1 30.6 %copy-start.3 = (bf16[2,128,128]{2,1,0:T(8,128)(2,1)S(1)}, bf16[2,128,128]{2,1,0:T(8,128)(2,1)}, u32[]{:S(2)}) copy-start(bf16[2,128,128]{2,1,0:T(8,128)(2,1)} %out_gate.3) | copy-start | bytes 196612
  2.2 30.6 %copy-start.4 = (bf16[2,128,128]{2,1,0:T(8,128)(2,1)S(1)}, bf16[2,128,128]{2,1,0:T(8,128)(2,1)}, u32[]{:S(2)}) copy-start(bf16[2,128,128]{2,1,0:T(8,128)(2,1)} %out_weight.3) | copy-start | bytes 196612
  2.2 30.6 %copy-start.5 = (s32[32,32]{1,0:T(8,128)S(1)}, s32[32,32]{1,0:T(8,128)}, u32[]{:S(2)}) copy-start(s32[32,32]{1,0:T(8,128)} %mask.1) | copy-start | bytes 12292
  2.2 30.6 %copy-start.7 = (f32[2,128]{1,0:T(2,128)S(1)}, f32[2,128]{1,0:T(2,128)}, u32[]{:S(2)}) copy-start(f32[2,128]{1,0:T(2,128)} %in_bias.3) | copy-start | bytes 3076
  2.2 30.6 %copy-start.8 = (f32[2,128]{1,0:T(2,128)S(1)}, f32[2,128]{1,0:T(2,128)}, u32[]{:S(2)}) copy-start(f32[2,128]{1,0:T(2,128)} %out_gain.1) | copy-start | bytes 3076
  2.2 30.6 %copy-start.9 = (f32[2,128]{1,0:T(2,128)S(1)}, f32[2,128]{1,0:T(2,128)}, u32[]{:S(2)}) copy-start(f32[2,128]{1,0:T(2,128)} %out_bias.1) | copy-start | bytes 3076
  31.6 3.0 %collective-permute-start = (bf16[128,16,128]{2,1,0:T(8,128)(2,1)S(1)}, bf16[128,16,128]{2,1,0:T(8,128)(2,1)S(1)}, u32[]{:S(2)}, u32[]{:S(2)}) collective-permute-start(bf16[128,16,128]{2,1,0:T(8,128)(2,1)S(1)} %all_to_all.20.own), channel_id=1, source_target_pairs={{0,1},{1,0},{2,3},{3,2},{4,5},{5,4},{6,7},{7,6},{8,9},{9,8},{10,11... | collective-permute-start | bytes 1572872 | tf_op jit(solution)/shard_map/ppermute | solution.py:279
  32.8 0.7 copy-start.6
  81.6 3.0 %collective-permute-start.1 = (bf16[128,16,128]{2,1,0:T(8,128)(2,1)S(1)}, bf16[128,16,128]{2,1,0:T(8,128)(2,1)S(1)}, u32[]{:S(2)}, u32[]{:S(2)}) collective-permute-start(bf16[128,16,128]{2,1,0:T(8,128)(2,1)S(1)} %all_to_all.22.own), channel_id=1, source_target_pairs={{0,1},{1,0},{2,3},{3,2},{4,5},{5,4},{6,7},{7,6},{8,9},{9,8},{10,11... | collective-permute-start | bytes 1572872 | tf_op jit(solution)/shard_map/ppermute | solution.py:279

commit v4 on v3

--- a/solution.py
+++ b/solution.py
@@ -24,7 +24,12 @@
     return min(x, 4 - x) + min(z, 8 - z) + min(y, 4 - y)
 
 
-PLACES = sorted(range(C), key=lambda place: (hops(place) > 0, -hops(place), away(place)))
+def turn(place):
+    x, z, y = away(place)
+    return hops(place) > 0, -hops(place), -x, -z, -y
+
+
+PLACES = sorted(range(C), key=turn)
 RANKS = {place: i for i, place in enumerate(PLACES)}
 GROUPS = [[2 * place + core for place in PLACES] for core in range(2)]
 VMEM_LIMIT = 32 * 1024 * 1024
@@ -185,6 +190,11 @@
             out[8 * q + s] = piece.astype(BF16)
 
 
+def regrouped(product):
+    quads = [jnp.split(part, product.shape[1] // C, axis=1) for part in jnp.split(product, 4)]
+    return jnp.concatenate([jnp.concatenate(parts, axis=1) for parts in zip(*quads)], axis=0)
+
+
 def outgoing_kernel(core, own, other, out, left, right):
     swap = swap_groups()
     half = core[0]
@@ -206,15 +216,12 @@
     pairs = right.reshape(8, 2, 4, 8, 512)
     b = jnp.concatenate([pairs[:, half, q].reshape(64, 512) for q in range(4)], axis=0)
     product = dot_nt(b.astype(BF16), a).astype(BF16)
-    for quad in range(4):
-        y = jnp.concatenate(
-            [product[64 * q : 64 * q + 64, quad * C : (quad + 1) * C] for q in range(4)], axis=1
-        )
-        z = dot(y, swap)
-        for r in range(4):
-            piece = z[:, r * C : (r + 1) * C].reshape(8, 8, C).astype(BF16)
-            for c in range(8):
-                out[rank(4 * quad + r, c)] = piece[c]
+    z = dot(regrouped(product), swap)
+    for r in range(16):
+        quad, lanes = r // 4, slice(r % 4 * C, (r % 4 + 1) * C)
+        piece = z[64 * quad : 64 * quad + 64, lanes].reshape(8, 8, C).astype(BF16)
+        for c in range(8):
+            out[rank(r, c)] = piece[c]
 
 
 def incoming_kernel(core, own, other, out, left, right):
@@ -238,17 +245,14 @@
     a = left[...].reshape(512, 512).astype(BF16)
     b = right[...].reshape(256, 512).astype(BF16)
     product = dot_nt(a, b).astype(BF16)
-    for quad in range(2):
-        y = jnp.concatenate(
-            [product[C * q : C * q + C, quad * C : (quad + 1) * C] for q in range(4)], axis=1
-        )
-        z = dot(y, swap)
-        for c in range(4):
-            piece = z[:, c * C : (c + 1) * C].reshape(2, 8, 8, C).astype(BF16)
-            for r in range(8):
-                even, odd = rank(2 * r, 4 * quad + c), rank(2 * r + 1, 4 * quad + c)
-                out[even + (odd - even) * half] = piece[0, r]
-                out[odd - (odd - even) * half] = piece[1, r]
+    z = dot(regrouped(product), swap)
+    for c in range(8):
+        quad, lanes = c // 4, slice(c % 4 * C, (c % 4 + 1) * C)
+        piece = z[C * quad : C * quad + C, lanes].reshape(2, 8, 8, C).astype(BF16)
+        for r in range(8):
+            even, odd = rank(2 * r, c), rank(2 * r + 1, c)
+            out[even + (odd - even) * half] = piece[0, r]
+            out[odd - (odd - even) * half] = piece[1, r]
 
 
 def call(kernel, out_shape, scratch, *args, smem=0, hbm=False):

time: 107 us -> 107 us (level)
  no operation moved by 1% of the time
where the time goes in v4:
time: 107 us; the launch traced here: 106 us
  blocking collectives  92.9 us (87%)
  Pallas kernels  9.36 us (9%)
  starting transfers between devices  3.11 us (3%)
    all_to_all x4, blocking collectives, exchange(): return lax.all_to_all(values, AXES, 0, 0, axis_index_groups=GROUPS)  92.9 us
    pallas_call x7, Pallas kernels, call(): pl.pallas_call(kernel, out_shape=out_shape, in_specs=[scalars] * smem + [...  9.36 us
    ppermute x2, starting transfers between devices, other_core(): return lax.ppermute(values, 'core', [(0, 1), (1, 0)])  3.11 us
  transfers between devices with their start and end apart: 2, of which 1 were waited for; matrix products, arithmetic and copies ran while one was open for 0% of the time, Pallas kernels for 2%

profile of v4, /device:TPU:1, one launch (start us, length us, event | category | flops | bytes accessed | tf_op | source)
XLA Modules:
  0.0 106.4 jit_solution(13077043302850380658)
XLA Ops:
  0.0 2.1 %shard_map.100 = bf16[128,16,128]{2,1,0:T(8,128)(2,1)S(1)} custom-call(bf16[32,32,128]{2,1,0:T(8,128)(2,1)} %pair, s32[32,32]{1,0:T(8,128)} %mask.1, f32[2,128]{1,0:T(2,128)} %in_gain.3, f32[2,128]{1,0:T(2,128)} %in_bias.3, bf16[2,128,256]{2,1,0:T(8,128)(2,1)} %weight.1, bf16[2,128,256]{2,1,0:T(8,128)(2,1)} %gate.1), custom_call_target="tpu_custom_call" | custom-call | tf_op jit(solution)/shard_map/pallas_call | solution.py:264
  2.1 0.0 copy-start
  2.1 0.0 copy-start.1
  2.1 0.0 copy-start.2
  2.1 0.0 copy-start.3
  2.2 0.0 copy-start.4
  2.2 0.0 copy-start.5
  2.2 0.0 copy-start.7
  2.2 0.0 copy-start.8
  2.2 0.0 copy-start.9
  2.2 29.5 %all_to_all.20.own = bf16[128,16,128]{2,1,0:T(8,128)(2,1)S(1)} all-to-all(bf16[128,16,128]{2,1,0:T(8,128)(2,1)S(1)} %shard_map.100), channel_id=1, replica_groups={{172,8,72,16,10,14,0,200,80,74,78,64,24,18,22,12,2,6,56,208,202,206,192..., dimensions={0} | all-to-all | bytes 1048576 | tf_op jit(solution)/shard_map/all_to_all | solution.py:279
  31.7 1.5 %collective-permute-start = (bf16[128,16,128]{2,1,0:T(8,128)(2,1)S(1)}, bf16[128,16,128]{2,1,0:T(8,128)(2,1)S(1)}, u32[]{:S(2)}, u32[]{:S(2)}) collective-permute-start(bf16[128,16,128]{2,1,0:T(8,128)(2,1)S(1)} %all_to_all.20.own), channel_id=1, source_target_pairs={{0,1},{1,0},{2,3},{3,2},{4,5},{5,4},{6,7},{7,6},{8,9},{9,8},{10,11... | collective-permute-start | bytes 1572872 | tf_op jit(solution)/shard_map/ppermute | solution.py:283
  33.2 0.0 copy-start.6
  33.3 0.0 copy-done
  33.3 0.0 copy-done.1
  33.3 0.0 copy-done.2
  33.3 0.0 copy-done.3
  33.3 0.0 copy-done.4
  33.3 0.0 copy-done.5
  33.3 0.0 copy-done.7
  33.3 0.0 copy-done.8
  33.3 0.0 copy-done.9
  33.3 0.6 copy-done.6
  33.9 1.2 %shard_map.101 = (f32[8,128,128]{2,1,0:T(8,128)S(1)}, f32[8,128,128]{2,1,0:T(8,128)S(1)}, bf16[512,128]{1,0:T(8,128)(2,1)S(1)}, bf16[128,128]{1,0:T(8,128)(2,1)S...) custom-call(bf16[32,32,128]{2,1,0:T(8,128)(2,1)S(1)} %copy-done, s32[32,32]{1,0:T(8,128)S(1)} %copy-done.5, ...), custom_call_target="tpu_custom_call" | custom-call | tf_op jit(solution)/shard_map/pallas_call | solution.py:264
  35.1 0.0 collective-permute-done.other
  35.1 1.2 %shard_map.102 = bf16[128,8,128]{2,1,0:T(8,128)(2,1)S(1)} custom-call(s32[1]{0:T(128)} %bitcast.core, bf16[128,16,128]{2,1,0:T(8,128)(2,1)S(1)} %all_to_all.20.own, bf16[128,16,128]{2,1,0:T(8,128)(2,1)S(1)} %collective-permute-done.other), custom_call_target="tpu_custom_call" | custom-call | tf_op jit(solution)/shard_map/pallas_call | solution.py:264
  36.4 19.4 %all_to_all.21.y = bf16[128,8,128]{2,1,0:T(8,128)(2,1)S(1)} all-to-all(bf16[128,8,128]{2,1,0:T(8,128)(2,1)S(1)} %shard_map.102), channel_id=1, replica_groups={{172,8,72,16,10,14,0,200,80,74,78,64,24,18,22,12,2,6,56,208,202,206,192..., dimensions={0} | all-to-all | bytes 524288 | tf_op jit(solution)/shard_map/all_to_all | solution.py:279
  55.8 1.0 shard_map.103
  56.8 24.8 %all_to_all.22.own = bf16[128,16,128]{2,1,0:T(8,128)(2,1)S(1)} all-to-all(bf16[128,16,128]{2,1,0:T(8,128)(2,1)S(1)} %get-tuple-element.33), channel_id=1, replica_groups={{172,8,72,16,10,14,0,200,80,74,78,64,24,18,22,12,2,6,56,208,202,206,192..., dimensions={0} | all-to-all | bytes 1048576 | tf_op jit(solution)/shard_map/all_to_all | solution.py:279
  81.6 1.6 %collective-permute-start.1 = (bf16[128,16,128]{2,1,0:T(8,128)(2,1)S(1)}, bf16[128,16,128]{2,1,0:T(8,128)(2,1)S(1)}, u32[]{:S(2)}, u32[]{:S(2)}) collective-permute-start(bf16[128,16,128]{2,1,0:T(8,128)(2,1)S(1)} %all_to_all.22.own), channel_id=1, source_target_pairs={{0,1},{1,0},{2,3},{3,2},{4,5},{5,4},{6,7},{7,6},{8,9},{9,8},{10,11... | collective-permute-start | bytes 1572872 | tf_op jit(solution)/shard_map/ppermute | solution.py:283
  83.2 1.3 %shard_map.104 = (f32[1024,128]{1,0:T(8,128)S(1)}, f32[1024,128]{1,0:T(8,128)S(1)}) custom-call(bf16[8,128,128]{2,1,0:T(8,128)(2,1)S(1)} %get-tuple-element.36.zt, f32[2,128]{1,0:T(2,128)S(1)} %copy-done.6, f32[2,128]{1,0:T(2,128)S(1)} %copy-done.7, bf16[2,128,128]{2,1,0:T(8,128)(2,1)S(1)} %copy-done.3), custom_call_target="tpu_custom_call" | custom-call | tf_op jit(solution)/shard_map/pallas_call | solution.py:264
  84.5 0.2 collective-permute-done.1.other
  84.7 1.3 %shard_map.105 = bf16[128,8,128]{2,1,0:T(8,128)(2,1)S(1)} custom-call(s32[1]{0:T(128)} %bitcast.core, bf16[128,16,128]{2,1,0:T(8,128)(2,1)S(1)} %all_to_all.22.own, bf16[128,16,128]{2,1,0:T(8,128)(2,1)S(1)} %collective-permute-done.1.other), custom_call_target="tpu_custom_call" | custom-call | tf_op jit(solution)/shard_map/pallas_call | solution.py:264
  86.1 19.2 %all_to_all.23.y = bf16[128,8,128]{2,1,0:T(8,128)(2,1)S(1)} all-to-all(bf16[128,8,128]{2,1,0:T(8,128)(2,1)S(1)} %shard_map.105), channel_id=1, replica_groups={{172,8,72,16,10,14,0,200,80,74,78,64,24,18,22,12,2,6,56,208,202,206,192..., dimensions={0} | all-to-all | bytes 524288 | tf_op jit(solution)/shard_map/all_to_all | solution.py:279
  105.2 1.2 %shard_map.106 = bf16[32,32,128]{2,1,0:T(8,128)(2,1)} custom-call(bf16[128,8,128]{2,1,0:T(8,128)(2,1)S(1)} %all_to_all.23.y, f32[1024,128]{1,0:T(8,128)S(1)} %get-tuple-element.39.z_in, f32[1024,128]{1,0:T(8,128)S(1)} %get-tuple-element.40.g_in, f32[6,128,128]{2,1,0:T(8,128)S(1)} %get-tuple-element.31.columns, bf16[2,128,128]{2,1,0:T(8,128)(2,1)S(1)} %copy-done.4), custom_call_target="tpu_custom_call" | custom-call | tf_op jit(solution)/shard_map/pallas_call | solution.py:264
Async XLA Ops:
  2.1 31.1 %copy-start = (bf16[32,32,128]{2,1,0:T(8,128)(2,1)S(1)}, bf16[32,32,128]{2,1,0:T(8,128)(2,1)}, u32[]{:S(2)}) copy-start(bf16[32,32,128]{2,1,0:T(8,128)(2,1)} %pair) | copy-start | bytes 786436
  2.1 31.1 %copy-start.1 = (bf16[2,128,256]{2,1,0:T(8,128)(2,1)S(1)}, bf16[2,128,256]{2,1,0:T(8,128)(2,1)}, u32[]{:S(2)}) copy-start(bf16[2,128,256]{2,1,0:T(8,128)(2,1)} %weight.1) | copy-start | bytes 393220
  2.1 31.1 %copy-start.2 = (bf16[2,128,256]{2,1,0:T(8,128)(2,1)S(1)}, bf16[2,128,256]{2,1,0:T(8,128)(2,1)}, u32[]{:S(2)}) copy-start(bf16[2,128,256]{2,1,0:T(8,128)(2,1)} %gate.1) | copy-start | bytes 393220
  2.1 31.1 %copy-start.3 = (bf16[2,128,128]{2,1,0:T(8,128)(2,1)S(1)}, bf16[2,128,128]{2,1,0:T(8,128)(2,1)}, u32[]{:S(2)}) copy-start(bf16[2,128,128]{2,1,0:T(8,128)(2,1)} %out_gate.3) | copy-start | bytes 196612
  2.2 31.1 %copy-start.4 = (bf16[2,128,128]{2,1,0:T(8,128)(2,1)S(1)}, bf16[2,128,128]{2,1,0:T(8,128)(2,1)}, u32[]{:S(2)}) copy-start(bf16[2,128,128]{2,1,0:T(8,128)(2,1)} %out_weight.3) | copy-start | bytes 196612
  2.2 31.1 %copy-start.5 = (s32[32,32]{1,0:T(8,128)S(1)}, s32[32,32]{1,0:T(8,128)}, u32[]{:S(2)}) copy-start(s32[32,32]{1,0:T(8,128)} %mask.1) | copy-start | bytes 12292
  2.2 31.1 %copy-start.7 = (f32[2,128]{1,0:T(2,128)S(1)}, f32[2,128]{1,0:T(2,128)}, u32[]{:S(2)}) copy-start(f32[2,128]{1,0:T(2,128)} %in_bias.3) | copy-start | bytes 3076
  2.2 31.1 %copy-start.8 = (f32[2,128]{1,0:T(2,128)S(1)}, f32[2,128]{1,0:T(2,128)}, u32[]{:S(2)}) copy-start(f32[2,128]{1,0:T(2,128)} %out_gain.1) | copy-start | bytes 3076
  2.2 31.1 %copy-start.9 = (f32[2,128]{1,0:T(2,128)S(1)}, f32[2,128]{1,0:T(2,128)}, u32[]{:S(2)}) copy-start(f32[2,128]{1,0:T(2,128)} %out_bias.1) | copy-start | bytes 3076
  31.7 3.4 %collective-permute-start = (bf16[128,16,128]{2,1,0:T(8,128)(2,1)S(1)}, bf16[128,16,128]{2,1,0:T(8,128)(2,1)S(1)}, u32[]{:S(2)}, u32[]{:S(2)}) collective-permute-start(bf16[128,16,128]{2,1,0:T(8,128)(2,1)S(1)} %all_to_all.20.own), channel_id=1, source_target_pairs={{0,1},{1,0},{2,3},{3,2},{4,5},{5,4},{6,7},{7,6},{8,9},{9,8},{10,11... | collective-permute-start | bytes 1572872 | tf_op jit(solution)/shard_map/ppermute | solution.py:283
  33.2 0.7 copy-start.6
  81.6 3.1 %collective-permute-start.1 = (bf16[128,16,128]{2,1,0:T(8,128)(2,1)S(1)}, bf16[128,16,128]{2,1,0:T(8,128)(2,1)S(1)}, u32[]{:S(2)}, u32[]{:S(2)}) collective-permute-start(bf16[128,16,128]{2,1,0:T(8,128)(2,1)S(1)} %all_to_all.22.own), channel_id=1, source_target_pairs={{0,1},{1,0},{2,3},{3,2},{4,5},{5,4},{6,7},{7,6},{8,9},{9,8},{10,11... | collective-permute-start | bytes 1572872 | tf_op jit(solution)/shard_map/ppermute | solution.py:283

commit v5 on v4

--- a/solution.py
+++ b/solution.py
@@ -90,12 +90,17 @@
 
 
 def first_kernel(
-    pair_hbm, mask_hbm, gain_hbm, bias_hbm, weight_hbm, gate_hbm, lr,
-    pair, mask, gain, bias, weight, gate, scratch, sems,
+    pair_hbm, mask_hbm, gain_hbm, bias_hbm, weight_hbm, gate_hbm,
+    out_gate_hbm, out_gain_hbm, out_bias_hbm, out_weight_hbm,
+    lr, pair, mask, gain, bias, weight, gate, out_gate, out_gain, out_bias, out_weight,
+    scratch, sems,
 ):
     moves = [
-        (weight_hbm.at[0], weight), (gate_hbm.at[0], gate), (mask_hbm, mask),
+        (weight_hbm.at[0], weight.at[0]), (gate_hbm.at[0], gate.at[0]), (mask_hbm, mask),
         (gain_hbm, gain), (bias_hbm, bias), (pair_hbm, pair),
+        (weight_hbm.at[1], weight.at[1]), (gate_hbm.at[1], gate.at[1]),
+        (out_gate_hbm, out_gate), (out_gain_hbm, out_gain),
+        (out_bias_hbm, out_bias), (out_weight_hbm, out_weight),
     ]
     copies = [pltpu.make_async_copy(a, b, sems.at[i]) for i, (a, b) in enumerate(moves)]
     for copy in copies:
@@ -103,10 +108,10 @@
     wide = jnp.where((iota((T, C), 1) & (T - 1)) == iota((T, C), 0), 1.0, 0.0).astype(BF16)
     for copy in copies[:3]:
         copy.wait()
-    weight_t = weight[...].T
-    gate_t = gate[...].T
+    weight_t = weight[0].T
+    gate_t = gate[0].T
     mask_rows = group_select(dot(mask[...].astype(F32).astype(BF16), wide))
-    for copy in copies[3:]:
+    for copy in copies[3:6]:
         copy.wait()
     normed = []
     for s in range(0, 8, 2):
@@ -116,6 +121,8 @@
     for s in range(0, 8, 2):
         emit_operands(dot_nt, weight_t, gate_t, normed[s // 2], mask_rows, scratch, s)
     lr[...] = scratch[...].reshape(C, 16, C).astype(BF16)
+    for copy in copies[6:]:
+        copy.wait()
 
 
 def first_side_kernel(
@@ -195,27 +202,33 @@
     return jnp.concatenate([jnp.concatenate(parts, axis=1) for parts in zip(*quads)], axis=0)
 
 
-def outgoing_kernel(core, own, other, out, left, right):
+def outgoing_sides(half, src, swap, left, right):
+    for quad in range(2):
+        y = jnp.concatenate(
+            [
+                jnp.concatenate([src[rank(r, 4 * quad + c)] for r in range(16)], axis=0)
+                for c in range(4)
+            ],
+            axis=1,
+        )
+        z = dot(y, swap).reshape(16, 16, 4 * C)
+        depth = pl.ds(quad * C, C)
+        for q in range(4):
+            left[:, q, :, depth] = z[:, :8, q * C : (q + 1) * C]
+            right[:, q, :, depth] = z[:, 8:, q * C : (q + 1) * C]
+    pairs = right.reshape(8, 2, 4, 8, 256)
+    b = jnp.concatenate([pairs[:, half, q].reshape(64, 256) for q in range(4)], axis=0)
+    return left[...].reshape(512, 256).astype(BF16), b.astype(BF16)
+
+
+def outgoing_own_kernel(core, own, a_out, b_out, left, right):
+    a_out[...], b_out[...] = outgoing_sides(core[0], own, swap_groups(), left, right)
+
+
+def outgoing_kernel(core, other, a_own, b_own, out, left, right):
     swap = swap_groups()
-    half = core[0]
-    for part, src in enumerate((own, other)):
-        for quad in range(2):
-            y = jnp.concatenate(
-                [
-                    jnp.concatenate([src[rank(r, 4 * quad + c)] for r in range(16)], axis=0)
-                    for c in range(4)
-                ],
-                axis=1,
-            )
-            z = dot(y, swap).reshape(16, 16, 4 * C)
-            depth = pl.ds((2 * part + quad) * C, C)
-            for q in range(4):
-                left[:, q, :, depth] = z[:, :8, q * C : (q + 1) * C]
-                right[:, q, :, depth] = z[:, 8:, q * C : (q + 1) * C]
-    a = left[...].reshape(512, 512).astype(BF16)
-    pairs = right.reshape(8, 2, 4, 8, 512)
-    b = jnp.concatenate([pairs[:, half, q].reshape(64, 512) for q in range(4)], axis=0)
-    product = dot_nt(b.astype(BF16), a).astype(BF16)
+    a, b = outgoing_sides(core[0], other, swap, left, right)
+    product = (dot_nt(b_own[...], a_own[...]) + dot_nt(b, a)).astype(BF16)
     z = dot(regrouped(product), swap)
     for r in range(16):
         quad, lanes = r // 4, slice(r % 4 * C, (r % 4 + 1) * C)
@@ -224,35 +237,43 @@
             out[rank(r, c)] = piece[c]
 
 
-def incoming_kernel(core, own, other, out, left, right):
+def incoming_sides(src, swap, left, right):
+    for quad in range(4):
+        y = jnp.concatenate(
+            [
+                jnp.concatenate([src[rank(4 * quad + r, c)] for c in range(8)], axis=0)
+                for r in range(4)
+            ],
+            axis=1,
+        )
+        z = dot(y, swap).reshape(8, 16, 4 * C)
+        depth = pl.ds(quad * C, C)
+        for q in range(4):
+            left[q, :, :, depth] = z[:, :8, q * C : (q + 1) * C]
+            if right is not None:
+                right[:, q, :, depth] = z[:, 8:, q * C : (q + 1) * C]
+    return left[...].reshape(256, 512).astype(BF16)
+
+
+def incoming_own_kernel(own, a_out, b_out, left, right):
+    a_out[...] = incoming_sides(own, swap_groups(), left, right)
+    b_out[...] = right[...].reshape(256, 512).astype(BF16)
+
+
+def incoming_kernel(core, other, a_own, b_own, out, left):
     swap = swap_groups()
     half = core[0]
-    for part, src in enumerate((own, other)):
-        for quad in range(4):
-            y = jnp.concatenate(
-                [
-                    jnp.concatenate([src[rank(4 * quad + r, c)] for c in range(8)], axis=0)
-                    for r in range(4)
-                ],
-                axis=1,
-            )
-            z = dot(y, swap).reshape(8, 16, 4 * C)
-            depth = pl.ds(quad * C, C)
-            for q in range(4):
-                left[q, part, :, :, depth] = z[:, :8, q * C : (q + 1) * C]
-                if part == 0:
-                    right[:, q, :, depth] = z[:, 8:, q * C : (q + 1) * C]
-    a = left[...].reshape(512, 512).astype(BF16)
-    b = right[...].reshape(256, 512).astype(BF16)
-    product = dot_nt(a, b).astype(BF16)
-    z = dot(regrouped(product), swap)
+    sides = (a_own[...], incoming_sides(other, swap, left, None))
+    products = [dot_nt(a, b_own[...]).astype(BF16) for a in sides]
+    z = dot(jnp.concatenate([regrouped(product) for product in products], axis=0), swap)
     for c in range(8):
-        quad, lanes = c // 4, slice(c % 4 * C, (c % 4 + 1) * C)
-        piece = z[C * quad : C * quad + C, lanes].reshape(2, 8, 8, C).astype(BF16)
+        lanes = slice(c % 4 * C, (c % 4 + 1) * C)
+        starts = [C * part + 64 * (c // 4) for part in range(2)]
+        piece = [z[i : i + 64, lanes].reshape(8, 8, C).astype(BF16) for i in starts]
         for r in range(8):
             even, odd = rank(2 * r, c), rank(2 * r + 1, c)
-            out[even + (odd - even) * half] = piece[0, r]
-            out[odd - (odd - even) * half] = piece[1, r]
+            out[even + (odd - even) * half] = piece[0][r]
+            out[odd - (odd - even) * half] = piece[1][r]
 
 
 def call(kernel, out_shape, scratch, *args, smem=0, hbm=False):
@@ -290,20 +311,24 @@
     operands = struct((C, 16, C), BF16)
     slabs = struct((8, C, C), F32)
     rows = struct((T * T, C), F32)
-    sides = [pltpu.VMEM((16, 4, 8, 512), F32), pltpu.VMEM((16, 4, 8, 512), F32)]
-
-    lr = call(
-        first_kernel, operands,
-        [
-            pltpu.VMEM((T, T, C), BF16), pltpu.VMEM((T, T), jnp.int32),
-            pltpu.VMEM((2, C), F32), pltpu.VMEM((2, C), F32),
-            pltpu.VMEM((C, 2 * C), BF16), pltpu.VMEM((C, 2 * C), BF16),
-            pltpu.VMEM((16 * C, C), F32), pltpu.SemaphoreType.DMA((6,)),
-        ],
-        pair, pair_mask, in_gain, in_bias, weight, gate, hbm=True,
-    )
-    own, side_pair = lax.optimization_barrier((exchange(lr), pair))
+    sides = [pltpu.VMEM((16, 4, 8, 256), F32), pltpu.VMEM((16, 4, 8, 256), F32)]
+
+    arguments = (
+        pair, pair_mask, in_gain, in_bias, weight, gate, out_gate, out_gain, out_bias, out_weight
+    )
+    (
+        lr, pair, pair_mask, in_gain, in_bias, weight, gate, out_gate, out_gain, out_bias, out_weight
+    ) = call(
+        first_kernel, [operands] + [struct(array.shape, array.dtype) for array in arguments],
+        [pltpu.VMEM((16 * C, C), F32), pltpu.SemaphoreType.DMA((12,))],
+        *arguments, hbm=True,
+    )
+    own = exchange(lr)
     other = other_core(own)
+    a_own, b_own = call(
+        outgoing_own_kernel, [struct((512, 256), BF16), struct((256, 256), BF16)], sides,
+        core, own, smem=1,
+    )
     zt, gt, weight_t, out_weight_t, columns, mask_rows = call(
         first_side_kernel,
         [
@@ -311,13 +336,12 @@
             struct((6, C, C), F32), struct((8, C), F32),
         ],
         [pltpu.VMEM((T * T, C), F32)],
-        side_pair, pair_mask, in_gain, in_bias, weight, gate, out_gate, out_gain, out_bias,
+        pair, pair_mask, in_gain, in_bias, weight, gate, out_gate, out_gain, out_bias,
         out_weight,
     )
-    other, zt = lax.optimization_barrier((other, zt))
+    other, zt, a_own = lax.optimization_barrier((other, zt, a_own))
     y = call(
-        outgoing_kernel, struct((C, 8, C), BF16), sides,
-        core, own, other, smem=1,
+        outgoing_kernel, struct((C, 8, C), BF16), sides, core, other, a_own, b_own, smem=1
     )
     y = exchange(y)
     lr, zt = call(
@@ -328,11 +352,14 @@
     own, zt = lax.optimization_barrier((exchange(lr), zt))
     other = other_core(own)
     z, g = call(second_side_kernel, [rows, rows], [], zt, in_gain, in_bias, out_gate)
-    other, z = lax.optimization_barrier((other, z))
+    left = pltpu.VMEM((4, 8, 8, 512), F32)
+    a_own, b_own = call(
+        incoming_own_kernel, [struct((256, 512), BF16), struct((256, 512), BF16)],
+        [left, pltpu.VMEM((8, 4, 8, 512), F32)], own,
+    )
+    other, z, a_own = lax.optimization_barrier((other, z, a_own))
     y = call(
-        incoming_kernel, struct((C, 8, C), BF16),
-        [pltpu.VMEM((4, 2, 8, 8, 512), F32), pltpu.VMEM((8, 4, 8, 512), F32)],
-        core, own, other, smem=1,
+        incoming_kernel, struct((C, 8, C), BF16), [left], core, other, a_own, b_own, smem=1
     )
     y = exchange(y)
     return call(

time: 107 us -> 106 us (level)
    pallas_call x7 -> x9, Pallas kernels: 9.36 us -> 9.69 us  [call(): pl.pallas_call(kernel, out_shape=out_shape, in_specs=[scalars] * smem + [...]
  transfers between devices with their start and end apart: 2 -> 2, of which waited for: 1 -> 0; matrix products, arithmetic and copies ran while one was open for 0% -> 0% of each run, Pallas kernels for 2% -> 3%
where the time goes in v5:
time: 106 us
  blocking collectives  92.7 us (87%)
  Pallas kernels  9.69 us (9%)
  starting transfers between devices  3.16 us (3%)
    all_to_all x4, blocking collectives, exchange(): return lax.all_to_all(values, AXES, 0, 0, axis_index_groups=GROUPS)  92.7 us
    pallas_call x9, Pallas kernels, call(): pl.pallas_call(kernel, out_shape=out_shape, in_specs=[scalars] * smem + [...  9.69 us
    ppermute x2, starting transfers between devices, other_core(): return lax.ppermute(values, 'core', [(0, 1), (1, 0)])  3.16 us
  transfers between devices with their start and end apart: 2, of which 0 were waited for; matrix products, arithmetic and copies ran while one was open for 0% of the time, Pallas kernels for 3%

profile of v5, /device:TPU:1, one launch (start us, length us, event | category | flops | bytes accessed | tf_op | source)
XLA Modules:
  0.0 105.7 jit_solution(8842715369642121087)
XLA Ops:
  0.0 2.2 %shard_map.100 = (bf16[128,16,128]{2,1,0:T(8,128)(2,1)S(1)}, bf16[32,32,128]{2,1,0:T(8,128)(2,1)S(1)}, s32[32,32]{1,0:T(8,128)S(1)}, f32[2,128]{1,0:T(2,128)S(1)...) custom-call(bf16[32,32,128]{2,1,0:T(8,128)(2,1)} %pair_hbm.1, ...), custom_call_target="tpu_custom_call" | custom-call | tf_op jit(solution)/shard_map/pallas_call | solution.py:285
  2.2 29.4 %all_to_all.20.own = bf16[128,16,128]{2,1,0:T(8,128)(2,1)S(1)} all-to-all(bf16[128,16,128]{2,1,0:T(8,128)(2,1)S(1)} %get-tuple-element.38), channel_id=1, replica_groups={{172,8,72,16,10,14,0,200,80,74,78,64,24,18,22,12,2,6,56,208,202,206,192..., dimensions={0} | all-to-all | bytes 1048576 | tf_op jit(solution)/shard_map/all_to_all | solution.py:300
  31.6 1.5 %collective-permute-start = (bf16[128,16,128]{2,1,0:T(8,128)(2,1)S(1)}, bf16[128,16,128]{2,1,0:T(8,128)(2,1)S(1)}, u32[]{:S(2)}, u32[]{:S(2)}) collective-permute-start(bf16[128,16,128]{2,1,0:T(8,128)(2,1)S(1)} %all_to_all.20.own), channel_id=1, source_target_pairs={{0,1},{1,0},{2,3},{3,2},{4,5},{5,4},{6,7},{7,6},{8,9},{9,8},{10,11... | collective-permute-start | bytes 1572872 | tf_op jit(solution)/shard_map/ppermute | solution.py:304
  33.1 1.2 %shard_map.101 = (f32[8,128,128]{2,1,0:T(8,128)S(1)}, f32[8,128,128]{2,1,0:T(8,128)S(1)}, bf16[512,128]{1,0:T(8,128)(2,1)S(1)}, bf16[128,128]{1,0:T(8,128)(2,1)S...) custom-call(bf16[32,32,128]{2,1,0:T(8,128)(2,1)S(1)} %get-tuple-element.39.pair, ...), custom_call_target="tpu_custom_call" | custom-call | tf_op jit(solution)/shard_map/pallas_call | solution.py:285
  34.3 0.5 shard_map.102
  34.8 0.0 collective-permute-done.other
  34.8 0.9 shard_map.103
  35.7 19.3 %all_to_all.21.y = bf16[128,8,128]{2,1,0:T(8,128)(2,1)S(1)} all-to-all(bf16[128,8,128]{2,1,0:T(8,128)(2,1)S(1)} %shard_map.103), channel_id=1, replica_groups={{172,8,72,16,10,14,0,200,80,74,78,64,24,18,22,12,2,6,56,208,202,206,192..., dimensions={0} | all-to-all | bytes 524288 | tf_op jit(solution)/shard_map/all_to_all | solution.py:300
  55.0 1.0 shard_map.104
  56.1 24.7 %all_to_all.22.own = bf16[128,16,128]{2,1,0:T(8,128)(2,1)S(1)} all-to-all(bf16[128,16,128]{2,1,0:T(8,128)(2,1)S(1)} %get-tuple-element.60), channel_id=1, replica_groups={{172,8,72,16,10,14,0,200,80,74,78,64,24,18,22,12,2,6,56,208,202,206,192..., dimensions={0} | all-to-all | bytes 1048576 | tf_op jit(solution)/shard_map/all_to_all | solution.py:300
  80.8 1.7 %collective-permute-start.1 = (bf16[128,16,128]{2,1,0:T(8,128)(2,1)S(1)}, bf16[128,16,128]{2,1,0:T(8,128)(2,1)S(1)}, u32[]{:S(2)}, u32[]{:S(2)}) collective-permute-start(bf16[128,16,128]{2,1,0:T(8,128)(2,1)S(1)} %all_to_all.22.own), channel_id=1, source_target_pairs={{0,1},{1,0},{2,3},{3,2},{4,5},{5,4},{6,7},{7,6},{8,9},{9,8},{10,11... | collective-permute-start | bytes 1572872 | tf_op jit(solution)/shard_map/ppermute | solution.py:304
  82.4 0.5 shard_map.106
  82.9 1.3 %shard_map.105 = (f32[1024,128]{1,0:T(8,128)S(1)}, f32[1024,128]{1,0:T(8,128)S(1)}) custom-call(bf16[8,128,128]{2,1,0:T(8,128)(2,1)S(1)} %get-tuple-element.63.zt, f32[2,128]{1,0:T(2,128)S(1)} %get-tuple-element.41.in_gain, f32[2,128]{1,0:T(2,128)S(1)} %get-tuple-element.42.in_bias, bf16[2,128,128]{2,1,0:T(8,128)(2,1)S(1)} %get-tuple-element.45.out_gate), custom_call_target="tpu_custom_call" | custom-call | tf_op jit(solution)/shard_map/pallas_call | solution.py:285
  84.2 0.0 collective-permute-done.1.other
  84.2 0.9 shard_map.107
  85.2 19.3 %all_to_all.23.y = bf16[128,8,128]{2,1,0:T(8,128)(2,1)S(1)} all-to-all(bf16[128,8,128]{2,1,0:T(8,128)(2,1)S(1)} %shard_map.107), channel_id=1, replica_groups={{172,8,72,16,10,14,0,200,80,74,78,64,24,18,22,12,2,6,56,208,202,206,192..., dimensions={0} | all-to-all | bytes 524288 | tf_op jit(solution)/shard_map/all_to_all | solution.py:300
  104.5 1.2 %shard_map.108 = bf16[32,32,128]{2,1,0:T(8,128)(2,1)} custom-call(bf16[128,8,128]{2,1,0:T(8,128)(2,1)S(1)} %all_to_all.23.y, f32[1024,128]{1,0:T(8,128)S(1)} %get-tuple-element.69.z_in, f32[1024,128]{1,0:T(8,128)S(1)} %get-tuple-element.70.g_in, f32[6,128,128]{2,1,0:T(8,128)S(1)} %get-tuple-element.58.columns, ...), custom_call_target="tpu_custom_call" | custom-call | tf_op jit(solution)/shard_map/pallas_call | solution.py:285
Async XLA Ops:
  31.6 3.2 %collective-permute-start = (bf16[128,16,128]{2,1,0:T(8,128)(2,1)S(1)}, bf16[128,16,128]{2,1,0:T(8,128)(2,1)S(1)}, u32[]{:S(2)}, u32[]{:S(2)}) collective-permute-start(bf16[128,16,128]{2,1,0:T(8,128)(2,1)S(1)} %all_to_all.20.own), channel_id=1, source_target_pairs={{0,1},{1,0},{2,3},{3,2},{4,5},{5,4},{6,7},{7,6},{8,9},{9,8},{10,11... | collective-permute-start | bytes 1572872 | tf_op jit(solution)/shard_map/ppermute | solution.py:304
  80.8 3.4 %collective-permute-start.1 = (bf16[128,16,128]{2,1,0:T(8,128)(2,1)S(1)}, bf16[128,16,128]{2,1,0:T(8,128)(2,1)S(1)}, u32[]{:S(2)}, u32[]{:S(2)}) collective-permute-start(bf16[128,16,128]{2,1,0:T(8,128)(2,1)S(1)} %all_to_all.22.own), channel_id=1, source_target_pairs={{0,1},{1,0},{2,3},{3,2},{4,5},{5,4},{6,7},{7,6},{8,9},{9,8},{10,11... | collective-permute-start | bytes 1572872 | tf_op jit(solution)/shard_map/ppermute | solution.py:304

commit v6 on v5

--- a/solution.py
+++ b/solution.py
@@ -81,9 +81,9 @@
     return jnp.where(src == back, 1.0, 0.0).astype(BF16)
 
 
-def emit_operands(multiply, weight_t, gate_t, normed, mask_rows, scratch, s):
+def emit_operands(projected, gate, mask_rows, scratch, s):
     masks = jnp.concatenate([mask_rows[s : s + 1], mask_rows[s + 1 : s + 2]], axis=1)
-    operands = sigmoid(multiply(gate_t, normed)) * multiply(weight_t, normed) * masks
+    operands = sigmoid(gate) * projected * masks
     for i in range(2):
         scratch[pl.ds(s + i, C, stride=16), :] = operands[:C, i * C : (i + 1) * C]
         scratch[pl.ds(8 + s + i, C, stride=16), :] = operands[C:, i * C : (i + 1) * C]
@@ -119,7 +119,8 @@
         x = normalize(jnp.concatenate(tokens, axis=0), 1)
         normed.append((x * gain[0:1, :] + bias[0:1, :]).astype(BF16))
     for s in range(0, 8, 2):
-        emit_operands(dot_nt, weight_t, gate_t, normed[s // 2], mask_rows, scratch, s)
+        tokens = normed[s // 2]
+        emit_operands(dot_nt(weight_t, tokens), dot_nt(gate_t, tokens), mask_rows, scratch, s)
     lr[...] = scratch[...].reshape(C, 16, C).astype(BF16)
     for copy in copies[6:]:
         copy.wait()
@@ -168,9 +169,8 @@
         z_out[s + 1] = z[:, C:]
         normed.append((normalize(z.astype(F32), 0) * twice[2] + twice[3]).astype(BF16))
     for s in range(0, 8, 2):
-        emit_operands(
-            dot, weight_t[: 2 * C], weight_t[2 * C :], normed[s // 2], mask_rows[...], scratch, s
-        )
+        both = dot(weight_t[...], normed[s // 2])
+        emit_operands(both[: 2 * C], both[2 * C :], mask_rows[...], scratch, s)
     lr[...] = scratch[...].reshape(C, 16, C).astype(BF16)
 
 

time: 106 us -> 106 us (level)
  no operation moved by 1% of the time
where the time goes in v6:
time: 106 us
  blocking collectives  92.7 us (87%)
  Pallas kernels  9.83 us (9%)
  starting transfers between devices  3.16 us (3%)
    all_to_all x4, blocking collectives, exchange(): return lax.all_to_all(values, AXES, 0, 0, axis_index_groups=GROUPS)  92.7 us
    pallas_call x9, Pallas kernels, call(): pl.pallas_call(kernel, out_shape=out_shape, in_specs=[scalars] * smem + [...  9.83 us
    ppermute x2, starting transfers between devices, other_core(): return lax.ppermute(values, 'core', [(0, 1), (1, 0)])  3.16 us
  transfers between devices with their start and end apart: 2, of which 0 were waited for; matrix products, arithmetic and copies ran while one was open for 0% of the time, Pallas kernels for 3%

profile of v6, /device:TPU:1, one launch (start us, length us, event | category | flops | bytes accessed | tf_op | source)
XLA Modules:
  0.0 105.8 jit_solution(16027074463934614820)
XLA Ops:
  0.0 2.2 %shard_map.100 = (bf16[128,16,128]{2,1,0:T(8,128)(2,1)S(1)}, bf16[32,32,128]{2,1,0:T(8,128)(2,1)S(1)}, s32[32,32]{1,0:T(8,128)S(1)}, f32[2,128]{1,0:T(2,128)S(1)...) custom-call(bf16[32,32,128]{2,1,0:T(8,128)(2,1)} %pair_hbm.1, ...), custom_call_target="tpu_custom_call" | custom-call | tf_op jit(solution)/shard_map/pallas_call | solution.py:285
  2.2 29.4 %all_to_all.20.own = bf16[128,16,128]{2,1,0:T(8,128)(2,1)S(1)} all-to-all(bf16[128,16,128]{2,1,0:T(8,128)(2,1)S(1)} %get-tuple-element.38), channel_id=1, replica_groups={{172,8,72,16,10,14,0,200,80,74,78,64,24,18,22,12,2,6,56,208,202,206,192..., dimensions={0} | all-to-all | bytes 1048576 | tf_op jit(solution)/shard_map/all_to_all | solution.py:300
  31.6 1.5 %collective-permute-start = (bf16[128,16,128]{2,1,0:T(8,128)(2,1)S(1)}, bf16[128,16,128]{2,1,0:T(8,128)(2,1)S(1)}, u32[]{:S(2)}, u32[]{:S(2)}) collective-permute-start(bf16[128,16,128]{2,1,0:T(8,128)(2,1)S(1)} %all_to_all.20.own), channel_id=1, source_target_pairs={{0,1},{1,0},{2,3},{3,2},{4,5},{5,4},{6,7},{7,6},{8,9},{9,8},{10,11... | collective-permute-start | bytes 1572872 | tf_op jit(solution)/shard_map/ppermute | solution.py:304
  33.1 1.2 %shard_map.101 = (f32[8,128,128]{2,1,0:T(8,128)S(1)}, f32[8,128,128]{2,1,0:T(8,128)S(1)}, bf16[512,128]{1,0:T(8,128)(2,1)S(1)}, bf16[128,128]{1,0:T(8,128)(2,1)S...) custom-call(bf16[32,32,128]{2,1,0:T(8,128)(2,1)S(1)} %get-tuple-element.39.pair, ...), custom_call_target="tpu_custom_call" | custom-call | tf_op jit(solution)/shard_map/pallas_call | solution.py:285
  34.3 0.5 shard_map.102
  34.8 0.0 collective-permute-done.other
  34.8 0.9 shard_map.103
  35.7 19.3 %all_to_all.21.y = bf16[128,8,128]{2,1,0:T(8,128)(2,1)S(1)} all-to-all(bf16[128,8,128]{2,1,0:T(8,128)(2,1)S(1)} %shard_map.103), channel_id=1, replica_groups={{172,8,72,16,10,14,0,200,80,74,78,64,24,18,22,12,2,6,56,208,202,206,192..., dimensions={0} | all-to-all | bytes 524288 | tf_op jit(solution)/shard_map/all_to_all | solution.py:300
  55.0 1.2 %shard_map.104 = (bf16[128,16,128]{2,1,0:T(8,128)(2,1)S(1)}, bf16[8,128,128]{2,1,0:T(8,128)(2,1)S(1)}) custom-call(bf16[128,8,128]{2,1,0:T(8,128)(2,1)S(1)} %all_to_all.21.y, f32[8,128,128]{2,1,0:T(8,128)S(1)} %get-tuple-element.54.zt, f32[8,128,128]{2,1,0:T(8,128)S(1)} %get-tuple-element.55.gt, bf16[512,128]{1,0:T(8,128)(2,1)S(1)} %get-tuple-element.56.weight_t, ...), custom_call_target="tpu_custom_call" | custom-call | tf_op jit(solution)/shard_map/pallas_call | solution.py:285
  56.2 24.7 %all_to_all.22.own = bf16[128,16,128]{2,1,0:T(8,128)(2,1)S(1)} all-to-all(bf16[128,16,128]{2,1,0:T(8,128)(2,1)S(1)} %get-tuple-element.60), channel_id=1, replica_groups={{172,8,72,16,10,14,0,200,80,74,78,64,24,18,22,12,2,6,56,208,202,206,192..., dimensions={0} | all-to-all | bytes 1048576 | tf_op jit(solution)/shard_map/all_to_all | solution.py:300
  80.9 1.7 %collective-permute-start.1 = (bf16[128,16,128]{2,1,0:T(8,128)(2,1)S(1)}, bf16[128,16,128]{2,1,0:T(8,128)(2,1)S(1)}, u32[]{:S(2)}, u32[]{:S(2)}) collective-permute-start(bf16[128,16,128]{2,1,0:T(8,128)(2,1)S(1)} %all_to_all.22.own), channel_id=1, source_target_pairs={{0,1},{1,0},{2,3},{3,2},{4,5},{5,4},{6,7},{7,6},{8,9},{9,8},{10,11... | collective-permute-start | bytes 1572872 | tf_op jit(solution)/shard_map/ppermute | solution.py:304
  82.6 0.5 shard_map.106
  83.1 1.3 %shard_map.105 = (f32[1024,128]{1,0:T(8,128)S(1)}, f32[1024,128]{1,0:T(8,128)S(1)}) custom-call(bf16[8,128,128]{2,1,0:T(8,128)(2,1)S(1)} %get-tuple-element.63.zt, f32[2,128]{1,0:T(2,128)S(1)} %get-tuple-element.41.in_gain, f32[2,128]{1,0:T(2,128)S(1)} %get-tuple-element.42.in_bias, bf16[2,128,128]{2,1,0:T(8,128)(2,1)S(1)} %get-tuple-element.45.out_gate), custom_call_target="tpu_custom_call" | custom-call | tf_op jit(solution)/shard_map/pallas_call | solution.py:285
  84.4 0.0 collective-permute-done.1.other
  84.4 0.9 shard_map.107
  85.3 19.3 %all_to_all.23.y = bf16[128,8,128]{2,1,0:T(8,128)(2,1)S(1)} all-to-all(bf16[128,8,128]{2,1,0:T(8,128)(2,1)S(1)} %shard_map.107), channel_id=1, replica_groups={{172,8,72,16,10,14,0,200,80,74,78,64,24,18,22,12,2,6,56,208,202,206,192..., dimensions={0} | all-to-all | bytes 524288 | tf_op jit(solution)/shard_map/all_to_all | solution.py:300
  104.6 1.2 %shard_map.108 = bf16[32,32,128]{2,1,0:T(8,128)(2,1)} custom-call(bf16[128,8,128]{2,1,0:T(8,128)(2,1)S(1)} %all_to_all.23.y, f32[1024,128]{1,0:T(8,128)S(1)} %get-tuple-element.69.z_in, f32[1024,128]{1,0:T(8,128)S(1)} %get-tuple-element.70.g_in, f32[6,128,128]{2,1,0:T(8,128)S(1)} %get-tuple-element.58.columns, ...), custom_call_target="tpu_custom_call" | custom-call | tf_op jit(solution)/shard_map/pallas_call | solution.py:285
Async XLA Ops:
  31.6 3.2 %collective-permute-start = (bf16[128,16,128]{2,1,0:T(8,128)(2,1)S(1)}, bf16[128,16,128]{2,1,0:T(8,128)(2,1)S(1)}, u32[]{:S(2)}, u32[]{:S(2)}) collective-permute-start(bf16[128,16,128]{2,1,0:T(8,128)(2,1)S(1)} %all_to_all.20.own), channel_id=1, source_target_pairs={{0,1},{1,0},{2,3},{3,2},{4,5},{5,4},{6,7},{7,6},{8,9},{9,8},{10,11... | collective-permute-start | bytes 1572872 | tf_op jit(solution)/shard_map/ppermute | solution.py:304
  80.9 3.4 %collective-permute-start.1 = (bf16[128,16,128]{2,1,0:T(8,128)(2,1)S(1)}, bf16[128,16,128]{2,1,0:T(8,128)(2,1)S(1)}, u32[]{:S(2)}, u32[]{:S(2)}) collective-permute-start(bf16[128,16,128]{2,1,0:T(8,128)(2,1)S(1)} %all_to_all.22.own), channel_id=1, source_target_pairs={{0,1},{1,0},{2,3},{3,2},{4,5},{5,4},{6,7},{7,6},{8,9},{9,8},{10,11... | collective-permute-start | bytes 1572872 | tf_op jit(solution)/shard_map/ppermute | solution.py:304

commit v7 on v5

--- a/solution.py
+++ b/solution.py
@@ -250,8 +250,7 @@
         depth = pl.ds(quad * C, C)
         for q in range(4):
             left[q, :, :, depth] = z[:, :8, q * C : (q + 1) * C]
-            if right is not None:
-                right[:, q, :, depth] = z[:, 8:, q * C : (q + 1) * C]
+            right[:, q, :, depth] = z[:, 8:, q * C : (q + 1) * C]
     return left[...].reshape(256, 512).astype(BF16)
 
 
@@ -260,11 +259,10 @@
     b_out[...] = right[...].reshape(256, 512).astype(BF16)
 
 
-def incoming_kernel(core, other, a_own, b_own, out, left):
+def incoming_kernel(core, a_other, a_own, b_own, out):
     swap = swap_groups()
     half = core[0]
-    sides = (a_own[...], incoming_sides(other, swap, left, None))
-    products = [dot_nt(a, b_own[...]).astype(BF16) for a in sides]
+    products = [dot_nt(a[...], b_own[...]).astype(BF16) for a in (a_own, a_other)]
     z = dot(jnp.concatenate([regrouped(product) for product in products], axis=0), swap)
     for c in range(8):
         lanes = slice(c % 4 * C, (c % 4 + 1) * C)
@@ -349,17 +347,16 @@
         [pltpu.VMEM((16 * C, C), F32), pltpu.VMEM((8 * C, C), F32)],
         y, zt, gt, weight_t, out_weight_t, columns, mask_rows,
     )
-    own, zt = lax.optimization_barrier((exchange(lr), zt))
-    other = other_core(own)
-    z, g = call(second_side_kernel, [rows, rows], [], zt, in_gain, in_bias, out_gate)
-    left = pltpu.VMEM((4, 8, 8, 512), F32)
     a_own, b_own = call(
         incoming_own_kernel, [struct((256, 512), BF16), struct((256, 512), BF16)],
-        [left, pltpu.VMEM((8, 4, 8, 512), F32)], own,
-    )
-    other, z, a_own = lax.optimization_barrier((other, z, a_own))
+        [pltpu.VMEM((4, 8, 8, 512), F32), pltpu.VMEM((8, 4, 8, 512), F32)], exchange(lr),
+    )
+    a_own, zt = lax.optimization_barrier((a_own, zt))
+    a_other = other_core(a_own)
+    z, g = call(second_side_kernel, [rows, rows], [], zt, in_gain, in_bias, out_gate)
+    a_other, z = lax.optimization_barrier((a_other, z))
     y = call(
-        incoming_kernel, struct((C, 8, C), BF16), [left], core, other, a_own, b_own, smem=1
+        incoming_kernel, struct((C, 8, C), BF16), [], core, a_other, a_own, b_own, smem=1
     )
     y = exchange(y)
     return call(

time: 106 us -> 106 us (level)
  no operation moved by 1% of the time
where the time goes in v7:
time: 106 us
  blocking collectives  92.7 us (87%)
  Pallas kernels  9.36 us (9%)
  starting transfers between devices  3.43 us (3%)
    all_to_all x4, blocking collectives, exchange(): return lax.all_to_all(values, AXES, 0, 0, axis_index_groups=GROUPS)  92.7 us
    pallas_call x9, Pallas kernels, call(): pl.pallas_call(kernel, out_shape=out_shape, in_specs=[scalars] * smem + [...  9.36 us
    ppermute x2, starting transfers between devices, other_core(): return lax.ppermute(values, 'core', [(0, 1), (1, 0)])  3.43 us
  transfers between devices with their start and end apart: 2, of which 0 were waited for; matrix products, arithmetic and copies ran while one was open for 0% of the time, Pallas kernels for 3%

profile of v7, /device:TPU:1, one launch (start us, length us, event | category | flops | bytes accessed | tf_op | source)
XLA Modules:
  0.0 105.6 jit_solution(2910778845657676137)
XLA Ops:
  0.0 2.2 %shard_map.100 = (bf16[128,16,128]{2,1,0:T(8,128)(2,1)S(1)}, bf16[32,32,128]{2,1,0:T(8,128)(2,1)S(1)}, s32[32,32]{1,0:T(8,128)S(1)}, f32[2,128]{1,0:T(2,128)S(1)...) custom-call(bf16[32,32,128]{2,1,0:T(8,128)(2,1)} %pair_hbm.1, ...), custom_call_target="tpu_custom_call" | custom-call | tf_op jit(solution)/shard_map/pallas_call | solution.py:283
  2.2 29.4 %all_to_all.20.own = bf16[128,16,128]{2,1,0:T(8,128)(2,1)S(1)} all-to-all(bf16[128,16,128]{2,1,0:T(8,128)(2,1)S(1)} %get-tuple-element.37), channel_id=1, replica_groups={{172,8,72,16,10,14,0,200,80,74,78,64,24,18,22,12,2,6,56,208,202,206,192..., dimensions={0} | all-to-all | bytes 1048576 | tf_op jit(solution)/shard_map/all_to_all | solution.py:298
  31.6 1.5 %collective-permute-start = (bf16[128,16,128]{2,1,0:T(8,128)(2,1)S(1)}, bf16[128,16,128]{2,1,0:T(8,128)(2,1)S(1)}, u32[]{:S(2)}, u32[]{:S(2)}) collective-permute-start(bf16[128,16,128]{2,1,0:T(8,128)(2,1)S(1)} %all_to_all.20.own), channel_id=1, source_target_pairs={{0,1},{1,0},{2,3},{3,2},{4,5},{5,4},{6,7},{7,6},{8,9},{9,8},{10,11... | collective-permute-start | bytes 1572872 | tf_op jit(solution)/shard_map/ppermute | solution.py:302
  33.1 1.2 %shard_map.101 = (f32[8,128,128]{2,1,0:T(8,128)S(1)}, f32[8,128,128]{2,1,0:T(8,128)S(1)}, bf16[512,128]{1,0:T(8,128)(2,1)S(1)}, bf16[128,128]{1,0:T(8,128)(2,1)S...) custom-call(bf16[32,32,128]{2,1,0:T(8,128)(2,1)S(1)} %get-tuple-element.38.pair, ...), custom_call_target="tpu_custom_call" | custom-call | tf_op jit(solution)/shard_map/pallas_call | solution.py:283
  34.3 0.5 shard_map.102
  34.8 0.0 collective-permute-done.other
  34.8 0.9 shard_map.103
  35.7 19.3 %all_to_all.21.y = bf16[128,8,128]{2,1,0:T(8,128)(2,1)S(1)} all-to-all(bf16[128,8,128]{2,1,0:T(8,128)(2,1)S(1)} %shard_map.103), channel_id=1, replica_groups={{172,8,72,16,10,14,0,200,80,74,78,64,24,18,22,12,2,6,56,208,202,206,192..., dimensions={0} | all-to-all | bytes 524288 | tf_op jit(solution)/shard_map/all_to_all | solution.py:298
  55.0 1.0 shard_map.104
  56.1 24.7 %all_to_all.22.own = bf16[128,16,128]{2,1,0:T(8,128)(2,1)S(1)} all-to-all(bf16[128,16,128]{2,1,0:T(8,128)(2,1)S(1)} %get-tuple-element.59), channel_id=1, replica_groups={{172,8,72,16,10,14,0,200,80,74,78,64,24,18,22,12,2,6,56,208,202,206,192..., dimensions={0} | all-to-all | bytes 1048576 | tf_op jit(solution)/shard_map/all_to_all | solution.py:298
  80.8 0.5 shard_map.105
  81.3 1.9 %collective-permute-start.1 = (bf16[256,512]{1,0:T(8,128)(2,1)S(1)}, bf16[256,512]{1,0:T(8,128)(2,1)S(1)}, u32[]{:S(2)}, u32[]{:S(2)}) collective-permute-start(bf16[256,512]{1,0:T(8,128)(2,1)S(1)} %get-tuple-element.62.a_own), channel_id=1, source_target_pairs={{0,1},{1,0},{2,3},{3,2},{4,5},{5,4},{6,7},{7,6},{8,9},{9,8},{10,11... | collective-permute-start | bytes 786440 | tf_op jit(solution)/shard_map/ppermute | solution.py:302
  83.2 1.3 %shard_map.106 = (f32[1024,128]{1,0:T(8,128)S(1)}, f32[1024,128]{1,0:T(8,128)S(1)}) custom-call(bf16[8,128,128]{2,1,0:T(8,128)(2,1)S(1)} %get-tuple-element.63.zt, f32[2,128]{1,0:T(2,128)S(1)} %get-tuple-element.40.in_gain, f32[2,128]{1,0:T(2,128)S(1)} %get-tuple-element.41.in_bias, bf16[2,128,128]{2,1,0:T(8,128)(2,1)S(1)} %get-tuple-element.44.out_gate), custom_call_target="tpu_custom_call" | custom-call | tf_op jit(solution)/shard_map/pallas_call | solution.py:283
  84.5 0.0 collective-permute-done.1.a_other
  84.5 0.6 shard_map.107
  85.1 19.3 %all_to_all.23.y = bf16[128,8,128]{2,1,0:T(8,128)(2,1)S(1)} all-to-all(bf16[128,8,128]{2,1,0:T(8,128)(2,1)S(1)} %shard_map.107), channel_id=1, replica_groups={{172,8,72,16,10,14,0,200,80,74,78,64,24,18,22,12,2,6,56,208,202,206,192..., dimensions={0} | all-to-all | bytes 524288 | tf_op jit(solution)/shard_map/all_to_all | solution.py:298
  104.4 1.2 %shard_map.108 = bf16[32,32,128]{2,1,0:T(8,128)(2,1)} custom-call(bf16[128,8,128]{2,1,0:T(8,128)(2,1)S(1)} %all_to_all.23.y, f32[1024,128]{1,0:T(8,128)S(1)} %get-tuple-element.67.z_in, f32[1024,128]{1,0:T(8,128)S(1)} %get-tuple-element.68.g_in, f32[6,128,128]{2,1,0:T(8,128)S(1)} %get-tuple-element.57.columns, ...), custom_call_target="tpu_custom_call" | custom-call | tf_op jit(solution)/shard_map/pallas_call | solution.py:283
Async XLA Ops:
  31.6 3.2 %collective-permute-start = (bf16[128,16,128]{2,1,0:T(8,128)(2,1)S(1)}, bf16[128,16,128]{2,1,0:T(8,128)(2,1)S(1)}, u32[]{:S(2)}, u32[]{:S(2)}) collective-permute-start(bf16[128,16,128]{2,1,0:T(8,128)(2,1)S(1)} %all_to_all.20.own), channel_id=1, source_target_pairs={{0,1},{1,0},{2,3},{3,2},{4,5},{5,4},{6,7},{7,6},{8,9},{9,8},{10,11... | collective-permute-start | bytes 1572872 | tf_op jit(solution)/shard_map/ppermute | solution.py:302
  81.3 3.2 %collective-permute-start.1 = (bf16[256,512]{1,0:T(8,128)(2,1)S(1)}, bf16[256,512]{1,0:T(8,128)(2,1)S(1)}, u32[]{:S(2)}, u32[]{:S(2)}) collective-permute-start(bf16[256,512]{1,0:T(8,128)(2,1)S(1)} %get-tuple-element.62.a_own), channel_id=1, source_target_pairs={{0,1},{1,0},{2,3},{3,2},{4,5},{5,4},{6,7},{7,6},{8,9},{9,8},{10,11... | collective-permute-start | bytes 786440 | tf_op jit(solution)/shard_map/ppermute | solution.py:302
